TPU v7x, 256 devices: a whole 4x4x8 slice. The times are simulated.
256 devices in a mesh: xy: 32 (over z, x_hi, core), gz: 8 (over x_lo, y).
Axes of the slice: x: 4 (x_hi: 2, x_lo: 2; x = x_hi * 2 + x_lo), y: 4, z: 8, core: 2. Of those that a mesh axis runs over, the one named last changes fastest.
Arguments:
- field_tiles: bfloat16 [32, 128, 128, 1024], P('xy', None, None, 'gz'), may hold values from -6 to 6
- core_x: bfloat16 [512, 192], replicated, may hold values from -0.25 to 0.25
- core_y: bfloat16 [1024, 192], replicated, may hold values from -0.1875 to 0.1875
- core_z: bfloat16 [1024, 192], P('gz'), may hold values from -0.1875 to 0.1875
- x_second: bfloat16 [512, 96], replicated, may hold values from -0.25 to 0.25
- x_third: bfloat16 [512, 96], replicated, may hold values from -0.25 to 0.25
- y_first: bfloat16 [1024, 96], replicated, may hold values from -0.1875 to 0.1875
- y_third: bfloat16 [1024, 96], replicated, may hold values from -0.1875 to 0.1875
- z_first: bfloat16 [1024, 96], P('gz'), may hold values from -0.1875 to 0.1875
- z_second: bfloat16 [1024, 96], P('gz'), may hold values from -0.1875 to 0.1875
Outputs:
- mode_one: float32 [512, 96], P(('xy', 'gz'))
- mode_two: float32 [1024, 96], P(('xy', 'gz'))
- mode_three: float32 [96, 1024], P('xy', 'gz')
- core_sketch: float32 [192, 192, 192], P('xy', None, 'gz')
All inputs are finite; a program needn't handle non-finite values.
Results may differ from a plain program's by a relative error of at most 0.007.
Values may be sent and summed in bfloat16 or wider, within the bound.
A program may use at most 128 MiB of HBM per device.

v0:
```python
import jax
import jax.numpy as jnp
from jax import lax
from jax.sharding import PartitionSpec as P

K = 96
TX = 128
TY = 128


def row_slice(matrix, offset, length):
    return lax.dynamic_slice_in_dim(matrix, offset, length, 0)


def shards(
    field_tiles, core_x, core_y, core_z, x_second, x_third, y_first, y_third, z_first, z_second
):
    tile_total = lax.axis_size("xy")
    column_tiles = tile_total // 4
    tile_index = lax.axis_index("xy")
    x_offset = tile_index // column_tiles * TX
    y_offset = tile_index % column_tiles * TY
    block_data = field_tiles[0]
    z_pair = jnp.concatenate([z_first, z_second], axis=1)
    paired = jnp.einsum("abz,zk->abk", block_data, z_pair, preferred_element_type=jnp.float32)
    g_one = jnp.sum(
        paired[:, :, :K] * row_slice(y_first, y_offset, TY).astype(jnp.float32)[None], axis=1
    )
    g_two = jnp.sum(
        paired[:, :, K:] * row_slice(x_second, x_offset, TX).astype(jnp.float32)[:, None], axis=0
    )
    first_full = lax.dynamic_update_slice_in_dim(
        jnp.zeros((x_second.shape[0], K), jnp.float32), g_one, x_offset, 0
    )
    second_full = lax.dynamic_update_slice_in_dim(
        jnp.zeros((y_first.shape[0], K), jnp.float32), g_two, y_offset, 0
    )
    mode_one, mode_two = (
        lax.psum_scatter(first_full, ("xy", "gz"), scatter_dimension=0, tiled=True),
        lax.psum_scatter(second_full, ("xy", "gz"), scatter_dimension=0, tiled=True),
    )
    across = jnp.einsum(
        "abz,ak->bkz",
        block_data,
        row_slice(x_third, x_offset, TX),
        preferred_element_type=jnp.float32,
    )
    g_three = jnp.sum(
        across * row_slice(y_third, y_offset, TY).astype(jnp.float32)[:, :, None], axis=0
    )
    mode_three = lax.psum_scatter(g_three, "xy", scatter_dimension=0, tiled=True)
    z_matrix = core_z.astype(jnp.float32)
    lowered = jnp.einsum(
        "abz,ap->pbz",
        block_data,
        row_slice(core_x, x_offset, TX),
        preferred_element_type=jnp.float32,
    ).astype(jnp.bfloat16)
    y_rows = row_slice(core_y, y_offset, TY)
    plane_part = lax.psum_scatter(
        jnp.einsum("pbz,bq->pqz", lowered, y_rows, preferred_element_type=jnp.float32),
        "xy",
        scatter_dimension=0,
        tiled=True,
    )
    partial_value = jnp.einsum("pqz,zr->pqr", plane_part, z_matrix, precision=lax.Precision.HIGHEST)
    core_sketch = lax.psum_scatter(partial_value, "gz", scatter_dimension=2, tiled=True)
    return (mode_one, mode_two, mode_three, core_sketch)


def solution(mesh):
    return jax.shard_map(
        shards,
        mesh=mesh,
        in_specs=(
            P("xy", None, None, "gz"),
            P(),
            P(),
            P("gz", None),
            P(),
            P(),
            P(),
            P(),
            P("gz", None),
            P("gz", None),
        ),
        out_specs=(
            P(("xy", "gz"), None),
            P(("xy", "gz"), None),
            P("xy", "gz"),
            P("xy", None, "gz"),
        ),
        check_vma=False,
    )
```

profile of v0, /device:TPU:1, one launch (start us, length us, event | category | flops | bytes accessed | tf_op | source)
XLA Modules:
  0.0 415.5 jit_solution(7495834419953925835)
XLA Ops:
  8.0 0.0 copy-start
  8.0 0.0 reduce-scatter.3.cloned.1.call-start
  8.1 5.9 %fusion.3 = bf16[192,128,128]{2,0,1:T(8,128)(2,1)S(1)} fusion(bf16[128,128,128]{2,1,0:T(8,128)(2,1)} %bitcast.28, bf16[512,192]{0,1:T(8,128)(2,1)} %param.11, s32[]{:T(128)S(6)} %select_n.26), kind=kOutput, calls=%fused_computation.9 | convolution fusion | flops 805306368 | bytes 10534916 | tf_op jit(solution)/shard_map/abz,ap->pbz/dot_general | solution.py:53
  14.0 0.0 copy-done
  14.0 17.9 %convolution_bitcast_fusion = f32[192,192,128]{2,1,0:T(8,128)} fusion(bf16[192,128,128]{2,0,1:T(8,128)(2,1)S(1)} %fusion.3, bf16[1024,192]{0,1:T(8,128)(2,1)S(1)} %copy-done, s32[]{:T(128)S(6)} %select_n.24), kind=kOutput, calls=%fused_computation.1 | convolution fusion | flops 1207959552 | bytes 25214980 | tf_op jit(solution)/shard_map/pbz,bq->pqz/dot_general | solution.py:61
  31.9 0.0 copy-start.4
  31.9 0.0 copy-start.5
  31.9 0.0 reduce-scatter.3.cloned.1.call-update
  31.9 0.2 all-reduce.6.cloned.1.call-start
  32.2 0.7 dynamic-slice_convert_fusion.1
  32.9 0.1 copy.17
  33.0 0.7 dynamic-slice_convert_fusion.2
  33.8 0.0 copy-done.4
  33.8 0.0 copy-done.5
  33.8 4.0 convolution_bitcast_fusion.1
  37.8 0.0 copy-start.3
  37.8 0.0 copy-start.6
  37.8 4.2 %fusion = (f32[128,96]{0,1:T(8,128)S(1)}, f32[128,96]{1,0:T(8,128)S(1)}) fusion(f32[128,128,192]{1,2,0:T(8,128)S(1)} %convolution_bitcast_fusion.1, f32[128,96]{1,0:T(8,128)S(1)} %copy.17, f32[128,96]{0,1:T(8,128)S(1)} %dynamic-slice_convert_fusion.2), kind=kLoop, calls=%fused_computation.3 | loop fusion | flops 6266880 | bytes 12779520 | tf_op jit(solution)/shard_map/reduce_sum | solution.py:29
  42.0 0.1 copy.18
  42.2 0.0 copy-start.1
  42.2 0.0 copy-start.2
  42.2 0.7 copy-done.1
  43.0 0.1 copy-done.2
  43.1 0.0 all-reduce.6.cloned.1.call-update
  43.1 0.0 reduce-scatter.5.cloned.1.call-start
  43.2 224.3 %reduce-scatter.3.cloned.1.call-done = f32[6,192,128]{2,1,0:T(8,128)} async-done(((f32[192,192,128]{2,1,0:T(8,128)}), f32[6,192,128]{2,1,0:T(8,128)}) %reduce-scatter.3.cloned.1.call-update) | async-done | bytes 589840 | tf_op jit(solution)/shard_map/reduce_scatter | solution.py:60
  267.5 0.0 copy-done.3
  267.5 2.7 fusion.11
  270.2 0.0 reduce-scatter.5.cloned.1.call-update
  270.3 0.8 dynamic-slice_convert_fusion
  271.0 0.1 copy.20
  271.1 0.0 copy-done.6
  271.1 0.6 dynamic-slice.2
  272.4 6.1 %fusion.2 = f32[96,128]{1,0:T(8,128)S(1)} fusion(f32[128,96]{1,0:T(8,128)S(1)} %copy.20, bf16[128,128,128]{2,1,0:T(8,128)(2,1)} %bitcast.29, bf16[512,96]{0,1:T(8,128)(2,1)} %param.15, s32[]{:T(128)S(6)} %select_n.26), kind=kOutput, calls=%fused_computation.7 | convolution fusion | flops 405786624 | bytes 4317188 | tf_op jit(solution)/shard_map/abz,ak->bkz/dot_general | solution.py:42
  278.4 126.6 %all-reduce.2 = f32[96,128]{1,0:T(8,128)S(1)} all-reduce(f32[96,128]{1,0:T(8,128)S(1)} %fusion.2), channel_id=4, replica_groups=mesh['xy'=32,'gz'=8] {'xy'}, use_global_device_ids=true, to_apply=%region_5.6.clone | all-reduce | flops 12288 | bytes 98304
  405.0 0.6 constant_dynamic-slice_fusion
  405.6 0.0 all-reduce.6.cloned.1.call-done
  405.6 1.2 constant_dynamic-slice_fusion.2
  406.8 1.3 constant_dynamic-slice_fusion.1
  408.1 0.0 reduce-scatter.5.cloned.1.call-done
  (4 shorter events, 0.1 us)
Async XLA Ops:
  8.0 6.0 %copy-start = (bf16[1024,192]{0,1:T(8,128)(2,1)S(1)}, bf16[1024,192]{0,1:T(8,128)(2,1)}, u32[]{:S(2)}) copy-start(bf16[1024,192]{0,1:T(8,128)(2,1)} %param.12) | copy-start | bytes 1179652
  8.0 259.5 %reduce-scatter.3.cloned.1.call-start = ((), (), s32[]{:S(2)}) async-start(), calls=%async_computation.2 | async-start | bytes 19464192 | tf_op jit(solution)/shard_map/reduce_scatter | solution.py:60
  31.9 1.9 copy-start.4
  31.9 1.9 copy-start.5
  31.9 373.7 %all-reduce.6.cloned.1.call-start = ((), (), s32[]{:S(2)}) async-start(), calls=%async_computation.4 | async-start | bytes 1572864
  37.8 229.7 %copy-start.3 = (bf16[128,192]{0,1:T(8,128)(2,1)S(1)}, bf16[128,192]{0,1:T(8,128)(2,1)}, u32[]{:S(2)}) copy-start(bf16[128,192]{0,1:T(8,128)(2,1)} %param.13) | copy-start | bytes 147460
  37.8 233.3 %copy-start.6 = (u32[256]{0:T(256)S(1)}, u32[256]{0:T(256)}, u32[]{:S(2)}) copy-start(u32[256]{0:T(256)} %constant.52) | copy-start | bytes 3076
  42.2 0.8 copy-start.1
  42.2 0.9 copy-start.2
  43.1 365.0 %reduce-scatter.5.cloned.1.call-start = ((), (), s32[]{:S(2)}) async-start(), calls=%async_computation.3 | async-start | bytes 1327104 | tf_op jit(solution)/shard_map/reduce_scatter | solution.py:67
Sparse Core Ops, SparseCore 0:
  32.1 235.3 reduce-scatter.2
  270.8 38.2 reduce-scatter.4
Sparse Core Ops, SparseCore 1:
  43.2 283.0 all-reduce.5
where the time goes:
time: 420 us; the launch traced here: 416 us
  waiting for transfers between devices  224 us (53%)
  blocking collectives  127 us (30%)
  matrix products  36.6 us (9%)
  between operations  16.3 us (4%)
  other arithmetic  6.47 us (2%)
  local copies, waits for them, and re-layouts  4.9 us (1%)
    reduce_scatter x1, waiting for transfers between devices, shards(): lax.psum_scatter(jnp.einsum('pbz,bq->pqz', lowered, y_rows, preferred_ele...  224 us
    unnamed x1, blocking collectives  127 us
    dot_general x1, matrix products, shards(): jnp.einsum('pbz,bq->pqz', lowered, y_rows, preferred_element_type=jnp.flo...  17.9 us
  transfers between devices with their start and end apart: 3, of which 1 were waited for; matrix products, arithmetic and copies ran while one was open for 6% of the time, Pallas kernels for 0%

commit v1 on v0

v1 whole, which is shorter than its diff:
```python
import functools

import jax
import jax.numpy as jnp
import numpy as np
from jax import lax
from jax.experimental import pallas as pl
from jax.experimental.pallas import tpu as pltpu
from jax.sharding import PartitionSpec as P

MESH = pl.DeviceIdType.MESH
F32, BF16 = jnp.float32, jnp.bfloat16
K = 96
S = 192
T = 128
CH = 16
NCH = T // CH
ROWS = 9 * CH


def one_hot(rows, columns, pairs):
    m = np.zeros((rows, columns), np.float32)
    for r, c in pairs:
        m[r, c] = 1.0
    return m


def tables():
    r_of = lambda c, h, e, i: 24 * ((e // 4 % 2) * 4 + e % 4) + 12 * (e // 8) + 6 * c + 3 * h + i
    rsel = np.stack(
        [
            one_hot(96, S, [(h * 48 + e * 3 + i, r_of(c, h, e, i)) for h in range(2) for e in range(16) for i in range(3)])
            for c in range(2)
        ]
    )
    qsel = np.stack(
        [
            one_hot(S, 256, [(q, q) for q in range(S)]),
            one_hot(S, 256, [(q, q if q < 128 else q + 64) for q in range(S)]),
        ]
    )
    psel = one_hot(256, S, [(8 * t + i, 6 * t + i) for t in range(32) for i in range(6)])
    ksel = one_hot(256, K, [(8 * t + i, 3 * t + i) for t in range(32) for i in range(3)])
    zsel = np.stack([one_hot(K, 256, [(k, k) for k in range(K)]), one_hot(K, 256, [(k, 128 + k) for k in range(K)])])
    eye = one_hot(K, 128, [(k, k) for k in range(K)])
    return [jnp.asarray(m, BF16) for m in (rsel, qsel, psel, ksel, zsel, eye)]


def nn(a, b):
    return lax.dot_general(a, b, (((1,), (0,)), ((), ())), preferred_element_type=F32)


def nt(a, b):
    return lax.dot_general(a, b, (((1,), (1,)), ((), ())), preferred_element_type=F32)


def core_kernel(
    field, core_x, core_y, core_z, x_second, x_third, y_first, y_third, z_first, z_second,
    rsel, qsel, psel, ksel, zsel, eye,
    out, g1, g2,
    own, par, wt, us, send, mid, ring, second, gath, hbuf, zrecv, fbuf, frecv, wy, zp, g3,
    own_sem, par_s, par_r, mid_s, mid_r, dir_s, dir_r, com_s, com_r, sec_s, sec_r, z_s, z_r, f_s, f_r,
):
    t, g = lax.axis_index("xy"), lax.axis_index("gz")
    z, s = lax.div(t, 4), lax.rem(t, 4)
    xh, c = lax.div(s, 2), lax.rem(s, 2)
    xl, y = lax.div(g, 4), lax.rem(g, 4)
    X = xh * 2 + xl
    u, v = lax.div(t, 8), lax.rem(t, 8)
    mate = t + 1 - 2 * c

    def ring_dev(d, q):
        tt = t + (1 - d) * 2 * (lax.div(q, 2) - xh)
        gg = g + (1 - d) * 4 * (lax.rem(q, 2) - xl) + d * (q - y)
        return (tt, gg)

    def place(d):
        return (1 - d) * X + d * y

    def step(p, k):
        return lax.rem(p + k, 4)

    def copy(src, dst, ss, rs, dev):
        return pltpu.make_async_remote_copy(
            src_ref=src, dst_ref=dst, send_sem=ss, recv_sem=rs, device_id=dev, device_id_type=MESH
        )

    def own_copy(ch):
        return pltpu.make_async_copy(field.at[0, pl.ds(ch * CH, CH)], own.at[ch], own_sem.at[ch])

    def par_copy(ch):
        return copy(field.at[0, pl.ds(ch * CH, CH)], par.at[ch], par_s.at[ch], par_r.at[ch], (mate, g))

    def mid_copy(ch, w):
        d = lax.rem(ch, 2)
        p = place(d)
        src = send.at[ch, pl.ds(step(p, 2) * 4 + 2 * w, 2)]
        return copy(src, mid.at[ch, w], mid_s.at[ch, w], mid_r.at[ch, w], ring_dev(d, step(p, 1 + 2 * w)))

    def part(ch, w, h):
        p = place(lax.rem(ch, 2))
        return send.at[ch, pl.ds(step(p, 1 + 2 * w) * 4 + 2 * h, 2)]

    def dir_copy(ch, w):
        d = lax.rem(ch, 2)
        dst = ring.at[ch, w, pl.ds(2 * (1 - w), 2)]
        return copy(part(ch, w, 1 - w), dst, dir_s.at[ch, w], dir_r.at[ch, w], ring_dev(d, step(place(d), 1 + 2 * w)))

    def com_copy(ch, w):
        d = lax.rem(ch, 2)
        dst = ring.at[ch, w, pl.ds(2 * w, 2)]
        return copy(part(ch, w, w), dst, com_s.at[ch, w], com_r.at[ch, w], ring_dev(d, step(place(d), 1 + 2 * w)))

    def sec_copy(ch, k):
        d = lax.rem(ch, 2)
        q = step(place(1 - d), k)
        src = send.at[ch, place(d) * 4 + q]
        return copy(src, second.at[ch, k - 1], sec_s.at[ch, k - 1], sec_r.at[ch, k - 1], ring_dev(1 - d, q))

    def z_copy(k):
        zz = lax.rem(z + k, 8)
        return copy(hbuf.at[zz], zrecv.at[k - 1], z_s.at[k - 1], z_r.at[k - 1], (zz * 4 + s, g))

    def f_copy(k):
        q = step(s, k)
        return copy(fbuf.at[q], frecv.at[k - 1], f_s.at[k - 1], f_r.at[k - 1], (z * 4 + q, g))

    def start_own(ch, _):
        own_copy(ch).start()
        return 0

    lax.fori_loop(0, NCH, start_own, 0)

    barrier = pltpu.get_barrier_semaphore()
    others = [ring_dev(0, step(X, 1)), ring_dev(0, step(X, 3))]
    others += [ring_dev(1, step(y, k)) for k in (1, 2, 3)]
    others += [(lax.rem(z + k, 8) * 4 + s, g) for k in range(1, 8)]
    others += [(z * 4 + step(s, k), g) for k in (1, 2, 3)]
    for dev in others:
        pl.semaphore_signal(barrier, inc=1, device_id=dev, device_id_type=MESH)
    pl.semaphore_wait(barrier, len(others))

    def start_par(ch, _):
        par_copy(ch).start()
        return 0

    lax.fori_loop(0, NCH, start_par, 0)

    def rows(ref, base, n=T):
        return ref[pl.ds(pl.multiple_of(base, n), n), :]

    czt = nt(rsel[c], core_z[...]).astype(BF16)
    for h in range(2):
        wy[h, 0:T, :] = nn(rows(core_y, v * T), qsel[h]).astype(BF16)
        wy[h, T : 2 * T, :] = nn(rows(core_y, (v + 1 - 2 * c) * T), qsel[h]).astype(BF16)
    zp[...] = (nn(z_first[...], zsel[0]) + nn(z_second[...], zsel[1])).astype(BF16)
    y1 = nn(rows(y_first, v * T), eye[...])
    y3 = nt(eye[:, 0:K], rows(y_third, v * T))
    g2[...] = jnp.zeros_like(g2)
    g3[...] = jnp.zeros_like(g3)

    def contract(ch):
        own_copy(ch).wait()
        par_copy(ch).wait_recv()
        for a in range(CH):
            both = jnp.concatenate([own[ch, a], par[ch, a]], axis=0)
            w = nt(czt, both).astype(BF16)
            wt[0, a * 48 : a * 48 + 48, :] = w[0:48]
            wt[1, a * 48 : a * 48 + 48, :] = w[48:96]
        for b in range(4):
            top = nn(wt[0, b * 192 : b * 192 + 192, :], wy[0])
            bot = nn(wt[1, b * 192 : b * 192 + 192, :], wy[1])
            rest = top[:, 128:] + bot[:, 128:]
            for a in range(4):
                at = (b * 4 + a) * ROWS
                us[at : at + 48, :] = top[a * 48 : a * 48 + 48, 0:128]
                us[at + 48 : at + 96, :] = bot[a * 48 : a * 48 + 48, 0:128]
                us[at + 96 : at + 144, :] = rest[a * 48 : a * 48 + 48]
        d = lax.rem(ch, 2)

        def reorder(e, _):
            q = (1 - d) * e + d * (lax.rem(e, 4) * 4 + lax.div(e, 4))
            for kind in range(3):
                for i in range(3):
                    j = kind * 3 + i
                    block = us[pl.ds(kind * 48 + i + e * 3, CH, stride=ROWS), :]
                    send[ch, q, j * CH : j * CH + CH, :] = block.astype(BF16)
            return 0

        lax.fori_loop(0, 16, reorder, 0, unroll=True)
        for w in range(2):
            mid_copy(ch, w).start()
            dir_copy(ch, w).start()

    def modes(ch):
        x2 = nn(rows(x_second, u * T + ch * CH, CH), eye[...])
        x3 = nt(eye[:, 0:K], rows(x_third, u * T + ch * CH, CH))
        total = g2[...]
        factors = []
        for a in range(CH):
            m = nn(own[ch, a], zp[...])
            g1[pl.ds(ch * CH + a, 1), :] = jnp.sum(m[:, 0:128] * y1, axis=0, keepdims=True)
            total = total + m[:, 128:] * x2[a : a + 1]
            factors.append((y3 * x3[:, a : a + 1]).astype(BF16))
        g2[...] = total
        g3[...] += nn(jnp.concatenate(factors, axis=1), own[ch].reshape(CH * T, T))

    def forward(ch):
        p = place(lax.rem(ch, 2))
        for w in range(2):
            mid_copy(ch, w).wait_recv()
            base = step(p, 1 + 2 * w) * 4 + 2 * w
            for h in range(2):
                mine = send[ch, base + h].astype(F32)
                send[ch, base + h] = (mine + mid[ch, w, h].astype(F32)).astype(BF16)
            com_copy(ch, w).start()

    def finish(ch):
        p = place(lax.rem(ch, 2))
        for w in range(2):
            dir_copy(ch, w).wait_recv()
            com_copy(ch, w).wait_recv()
        for b in range(4):
            tot = send[ch, p * 4 + b].astype(F32) + ring[ch, 0, b].astype(F32) + ring[ch, 1, b].astype(F32)
            send[ch, p * 4 + b] = tot.astype(BF16)
        for k in (1, 2, 3):
            sec_copy(ch, k).start()

    def turn(it, _):
        @pl.when(it < NCH)
        def _():
            contract(it)

        @pl.when((it >= 1) & (it < NCH + 1))
        def _():
            forward(it - 1)

        @pl.when(it < NCH)
        def _():
            modes(it)

        @pl.when(it >= 2)
        def _():
            finish(it - 2)

        return 0

    lax.fori_loop(0, NCH + 2, turn, 0)

    def collect(ch, _):
        d = lax.rem(ch, 2)
        for k in (1, 2, 3):
            sec_copy(ch, k).wait_recv()
        tot = send[ch, place(d) * 4 + place(1 - d)].astype(F32)
        for k in range(3):
            tot = tot + second[ch, k].astype(F32)
        tot = tot.astype(BF16)
        for j in range(9):
            gath[j, pl.ds(pl.multiple_of(ch * CH, CH), CH), :] = tot[j * CH : j * CH + CH]
        return 0

    lax.fori_loop(0, NCH, collect, 0)

    cxp = nt(psel[...], rows(core_x, u * T)).astype(BF16)
    for j in range(10):
        if j < 9:
            piece = nn(cxp, gath[j])
        else:
            piece = nn(ksel[...], g3[...].astype(BF16))
        hbuf[:, j * 32 : j * 32 + 32, :] = piece.astype(BF16).reshape(8, 32, T)
    for k in range(1, 8):
        z_copy(k).start()
    for k in range(1, 8):
        z_copy(k).wait_recv()
    for j in range(10):
        tot = hbuf[z, j * 32 : j * 32 + 32, :].astype(F32)
        for k in range(7):
            tot = tot + zrecv[k, j * 32 : j * 32 + 32, :].astype(F32)
        fbuf[:, j] = tot.reshape(4, 8, T)
    for k in (1, 2, 3):
        f_copy(k).start()
    out[s] = fbuf[s]
    for k in (1, 2, 3):
        f_copy(k).wait_recv()
        out[step(s, 4 - k)] = frecv[k - 1]

    def drain(ch, _):
        par_copy(ch).wait_send()
        for w in range(2):
            mid_copy(ch, w).wait_send()
            dir_copy(ch, w).wait_send()
            com_copy(ch, w).wait_send()
        for k in (1, 2, 3):
            sec_copy(ch, k).wait_send()
        return 0

    lax.fori_loop(0, NCH, drain, 0)
    for k in range(1, 8):
        z_copy(k).wait_send()
    for k in (1, 2, 3):
        f_copy(k).wait_send()


def mode_kernel(m, sel, one, two, recv, msg, r1, r2, a_s, a_r, b_s, b_r, c_s, c_r):
    t, g = lax.axis_index("xy"), lax.axis_index("gz")
    u, v = lax.div(t, 8), lax.rem(t, 8)

    def copy(src, dst, ss, rs, dev):
        return pltpu.make_async_remote_copy(
            src_ref=src, dst_ref=dst, send_sem=ss, recv_sem=rs, device_id=dev, device_id_type=MESH
        )

    def a_copy(k):
        q = lax.rem(g + k, 8)
        return copy(m.at[q], recv.at[k - 1], a_s.at[k - 1], a_r.at[k - 1], (t, q))

    def b_copy(k):
        q = lax.rem(v + k, 8)
        return copy(msg.at[q], r1.at[k - 1], b_s.at[k - 1], b_r.at[k - 1], (u * 8 + q, g))

    def c_send(b):
        return copy(msg.at[8 + b], r2.at[u], c_s.at[b], c_r.at[u], (v * 4 + b, g))

    def c_recv(k):
        return copy(msg.at[8], r2.at[k], c_s.at[0], c_r.at[k], (k * 8 + lax.div(t, 4), g))

    barrier = pltpu.get_barrier_semaphore()
    for k in range(1, 8):
        pl.semaphore_signal(barrier, inc=1, device_id=(t, lax.rem(g + k, 8)), device_id_type=MESH)
        pl.semaphore_signal(barrier, inc=1, device_id=(u * 8 + lax.rem(v + k, 8), g), device_id_type=MESH)
    for k in range(4):
        source = k * 8 + lax.div(t, 4)

        @pl.when(source != t)
        def _():
            pl.semaphore_signal(barrier, inc=1, device_id=(source, g), device_id_type=MESH)

    @pl.when(lax.div(t, 4) == v)
    def _():
        pl.semaphore_wait(barrier, 17)

    @pl.when(lax.div(t, 4) != v)
    def _():
        pl.semaphore_wait(barrier, 18)

    for k in range(1, 8):
        a_copy(k).start()
    total = m[g]
    for k in range(1, 8):
        a_copy(k).wait_recv()
        total = total + recv[k - 1]
    spread = lax.dot_general(
        sel[...], total, (((1,), (0,)), ((), ())), preferred_element_type=F32, precision=lax.Precision.HIGHEST
    )
    msg[...] = spread.reshape(12, 8, 128)
    for k in range(1, 8):
        b_copy(k).start()
    for b in range(4):

        @pl.when(v * 4 + b != t)
        def _():
            c_send(b).start()

        @pl.when(v * 4 + b == t)
        def _():
            r2[u] = msg[8 + b]

    first = msg[v]
    for k in range(1, 8):
        b_copy(k).wait_recv()
        first = first + r1[k - 1]
    one[...] = first
    for k in range(4):

        @pl.when(k * 8 + lax.div(t, 4) != t)
        def _():
            c_recv(k).wait_recv()

    two[...] = r2[0] + r2[1] + r2[2] + r2[3]
    for k in range(1, 8):
        a_copy(k).wait_send()
        b_copy(k).wait_send()
    for b in range(4):

        @pl.when(v * 4 + b != t)
        def _():
            c_send(b).wait_send()


def shards(*args):
    vm = pl.BlockSpec(memory_space=pltpu.VMEM)
    dma = pltpu.SemaphoreType.DMA
    out, g1, g2 = pl.pallas_call(
        core_kernel,
        out_shape=(
            jax.ShapeDtypeStruct((4, 10, 8, 128), F32),
            jax.ShapeDtypeStruct((T, 128), F32),
            jax.ShapeDtypeStruct((T, 128), F32),
        ),
        in_specs=[pl.BlockSpec(memory_space=pl.ANY)] + [vm] * 15,
        out_specs=(vm, vm, vm),
        scratch_shapes=[
            pltpu.VMEM((NCH, CH, T, T), BF16),
            pltpu.VMEM((NCH, CH, T, T), BF16),
            pltpu.VMEM((2, CH * 48, 256), BF16),
            pltpu.VMEM((CH * ROWS, 128), F32),
            pltpu.VMEM((NCH, 16, ROWS, 128), BF16),
            pltpu.VMEM((NCH, 2, 2, ROWS, 128), BF16),
            pltpu.VMEM((NCH, 2, 4, ROWS, 128), BF16),
            pltpu.VMEM((NCH, 3, ROWS, 128), BF16),
            pltpu.VMEM((9, T, 128), BF16),
            pltpu.VMEM((8, 320, 128), BF16),
            pltpu.VMEM((7, 320, 128), BF16),
            pltpu.VMEM((4, 10, 8, 128), F32),
            pltpu.VMEM((3, 10, 8, 128), F32),
            pltpu.VMEM((2, 2 * T, 256), BF16),
            pltpu.VMEM((T, 256), BF16),
            pltpu.VMEM((K, T), F32),
            dma((NCH,)), dma((NCH,)), dma((NCH,)),
            dma((NCH, 2)), dma((NCH, 2)), dma((NCH, 2)), dma((NCH, 2)), dma((NCH, 2)), dma((NCH, 2)),
            dma((NCH, 3)), dma((NCH, 3)), dma((7,)), dma((7,)), dma((3,)), dma((3,)),
        ],
        compiler_params=pltpu.CompilerParams(
            collective_id=0, has_side_effects=True, vmem_limit_bytes=56 * 1024 * 1024
        ),
    )(*args, *tables())

    first = g1.reshape(8, 8, 2, 128).transpose(1, 0, 2, 3).reshape(8, 16, 128)
    two = g2.reshape(4, 8, 4, 128).transpose(1, 0, 2, 3).reshape(8, 16, 128)
    sel = one_hot(96, 32, [(8 * h + i, 2 * h + i) for h in range(8) for i in range(2)]
                  + [(64 + 8 * h + i, 16 + 4 * h + i) for h in range(4) for i in range(4)])
    mode_one, mode_two = pl.pallas_call(
        mode_kernel,
        out_shape=(jax.ShapeDtypeStruct((8, 128), F32), jax.ShapeDtypeStruct((8, 128), F32)),
        in_specs=[vm, vm],
        out_specs=(vm, vm),
        scratch_shapes=[
            pltpu.VMEM((7, 32, 128), F32),
            pltpu.VMEM((12, 8, 128), F32),
            pltpu.VMEM((7, 8, 128), F32),
            pltpu.VMEM((4, 8, 128), F32),
            dma((7,)), dma((7,)), dma((7,)), dma((7,)), dma((4,)), dma((4,)),
        ],
        compiler_params=pltpu.CompilerParams(collective_id=1, has_side_effects=True),
    )(jnp.concatenate([first, two], axis=1), jnp.asarray(sel, F32))

    mode_three = jnp.sum(out[:, 9, 0:3], axis=0)
    core = out[:, 0:9].reshape(4, 3, 3, 8, 128)[:, :, :, 0:6]
    low = core[:, 0:2].transpose(3, 4, 0, 1, 2).reshape(6, 128, 24)
    high = core[:, 2].reshape(4, 3, 6, 2, 64).transpose(2, 4, 0, 3, 1).reshape(6, 64, 24)
    core_sketch = jnp.concatenate([low, high], axis=1)
    return (mode_one[0:2, 0:K], mode_two[0:4, 0:K], mode_three, core_sketch)


def solution(mesh):
    return jax.shard_map(
        shards,
        mesh=mesh,
        in_specs=(
            P("xy", None, None, "gz"),
            P(), P(), P("gz", None), P(), P(), P(), P(), P("gz", None), P("gz", None),
        ),
        out_specs=(
            P(("xy", "gz"), None),
            P(("xy", "gz"), None),
            P("xy", "gz"),
            P("xy", None, "gz"),
        ),
        check_vma=False,
    )
```

time: 420 us -> 111 us (0.26); the launches traced: 416 us -> 111 us
  waiting for transfers between devices: 224 us -> 0 us
  blocking collectives: 127 us -> 0 us
  Pallas kernels: 0 us -> 87 us
  matrix products: 36.6 us -> 0 us
  between operations: 16.3 us -> 0.72 us
  local copies, waits for them, and re-layouts: 4.9 us -> 20.4 us
    reduce_scatter x2 -> x0, waiting for transfers between devices: 224 us -> none  [the longest x1 224 us: shards(): lax.psum_scatter(jnp.einsum('pbz,bq->pqz', lowered, y_rows, preferred_ele...]
    unnamed x1 -> x0, blocking collectives: 127 us -> none
    pallas_call x0 -> x2, Pallas kernels: none -> 87 us  [the longest x1 72.3 us: shards(): pl.pallas_call(core_kernel, out_shape=(jax.ShapeDtypeStruct((4, 10, 8, 12...]
    dot_general x5 -> x0, matrix products: 36.6 us -> none  [the longest x1 17.9 us: shards(): jnp.einsum('pbz,bq->pqz', lowered, y_rows, preferred_element_type=jnp.flo...]
    unnamed x18 -> x11, local copies, waits for them, and re-layouts: 4.56 us -> 15 us
  transfers between devices with their start and end apart: 3 -> 0, of which waited for: 1 -> 0; matrix products, arithmetic and copies ran while one was open for 6% -> 0% of each run, Pallas kernels for 0% -> 0%
where the time goes in v1:
time: 111 us
  Pallas kernels  87 us (78%)
  local copies, waits for them, and re-layouts  20.4 us (18%)
  other arithmetic  2.65 us (2%)
    pallas_call x1, Pallas kernels, shards(): pl.pallas_call(core_kernel, out_shape=(jax.ShapeDtypeStruct((4, 10, 8, 12...  72.3 us
    unnamed x11, local copies, waits for them, and re-layouts  15 us
    pallas_call x1, Pallas kernels, shards(): pl.pallas_call(mode_kernel, out_shape=(jax.ShapeDtypeStruct((8, 128), F32...  14.7 us
    slice x2, local copies, waits for them, and re-layouts, shards(): return (mode_one[0:2, 0:K], mode_two[0:4, 0:K], mode_three, core_sketch)  2.49 us

profile of v1, /device:TPU:1, one launch (start us, length us, event | category | flops | bytes accessed | tf_op | source)
XLA Modules:
  0.0 110.8 jit_solution(17647597600467245299)
XLA Ops:
  0.6 1.4 %copy.41.z_first = bf16[128,96]{1,0:T(8,128)(2,1)} copy(bf16[128,96]{0,1:T(8,128)(2,1)} %param.25) | data formatting | bytes 49152 | tf_op args[8]
  2.1 1.4 %copy.42.z_second = bf16[128,96]{1,0:T(8,128)(2,1)} copy(bf16[128,96]{0,1:T(8,128)(2,1)} %param.26) | data formatting | bytes 49152 | tf_op args[9]
  3.5 1.5 %copy.36.core_z = bf16[128,192]{1,0:T(8,128)(2,1)} copy(bf16[128,192]{0,1:T(8,128)(2,1)} %param.20) | data formatting | bytes 98304 | tf_op args[3]
  5.0 1.7 %copy.37.x_second = bf16[512,96]{1,0:T(8,128)(2,1)} copy(bf16[512,96]{0,1:T(8,128)(2,1)} %param.21) | data formatting | bytes 196608 | tf_op args[4]
  6.7 1.6 %copy.38.x_third = bf16[512,96]{1,0:T(8,128)(2,1)} copy(bf16[512,96]{0,1:T(8,128)(2,1)} %param.22) | data formatting | bytes 196608 | tf_op args[5]
  8.3 1.8 %copy.34.core_x = bf16[512,192]{1,0:T(8,128)(2,1)} copy(bf16[512,192]{0,1:T(8,128)(2,1)} %param.18) | data formatting | bytes 393216 | tf_op args[1]
  10.1 1.8 %copy.39.y_first = bf16[1024,96]{1,0:T(8,128)(2,1)} copy(bf16[1024,96]{0,1:T(8,128)(2,1)} %param.23) | data formatting | bytes 393216 | tf_op args[6]
  11.9 1.8 %copy.40.y_third = bf16[1024,96]{1,0:T(8,128)(2,1)} copy(bf16[1024,96]{0,1:T(8,128)(2,1)} %param.24) | data formatting | bytes 393216 | tf_op args[7]
  13.6 2.0 %copy.35.core_y = bf16[1024,192]{1,0:T(8,128)(2,1)} copy(bf16[1024,192]{0,1:T(8,128)(2,1)} %param.19) | data formatting | bytes 786432 | tf_op args[2]
  15.6 72.3 %shard_map.192 = (f32[4,10,8,128]{3,2,1,0:T(8,128)}, f32[128,128]{1,0:T(8,128)}, f32[128,128]{1,0:T(8,128)}) custom-call(bf16[1,128,128,128]{3,2,1,0:T(8,128)(2,1)} %field.1, bf16[512,192]{1,0:T(8,128)(2,1)} %copy.34.core_x, bf16[1024,192]{1,0:T(8,128)(2,1)} %copy.35.core_y, bf16[128,192]{1,0:T(8,128)(2,1)} %copy.36.core_z, bf16[512,96]{1,0:T(8,128)(2,1)} %copy.37.x_second, ...), custom_call_target="tpu_custom_call" | custom-call | tf_op jit(solution)/shard_map/pallas_call | solution.py:393
  88.0 0.9 copy.43
  88.8 0.9 copy.44
  89.7 0.7 pad_maximum_fusion.1.m
  90.4 14.7 %shard_map.193 = (f32[8,128]{1,0:T(8,128)}, f32[8,128]{1,0:T(8,128)}) custom-call(f32[8,32,128]{2,1,0:T(8,128)} %pad_maximum_fusion.1.m, f32[96,32]{1,0:T(8,128)} %constant.22.clone.sel), custom_call_target="tpu_custom_call" | custom-call | tf_op jit(solution)/shard_map/pallas_call | solution.py:432
  105.0 1.2 %slice.21 = f32[2,96]{1,0:T(2,128)} slice(f32[8,128]{1,0:T(8,128)} %get-tuple-element.11), slice={[0:2], [0:96]} | slice | bytes 1536 | tf_op jit(solution)/shard_map/slice | solution.py:452
  106.3 1.2 %slice.22 = f32[4,96]{1,0:T(4,128)} slice(f32[8,128]{1,0:T(8,128)} %get-tuple-element.12), slice={[0:4], [0:96]} | slice | bytes 3072 | tf_op jit(solution)/shard_map/slice | solution.py:452
  107.5 1.3 %slice_reduce_fusion = f32[3,128]{1,0:T(4,128)} fusion(f32[4,10,8,128]{3,2,1,0:T(8,128)} %get-tuple-element.13), kind=kLoop, calls=%fused_computation.3 | loop fusion | flops 1152 | bytes 7680 | tf_op jit(solution)/shard_map/reduce_sum | solution.py:447
  108.8 0.9 slice.24
  109.9 0.1 reshape_squeeze.3
  110.1 0.7 pad_maximum_fusion
  (7 shorter events, 0.2 us)

commit v2 on v0

v2 whole, which is shorter than its diff:
```python
import jax
import jax.numpy as jnp
from jax import lax
from jax.experimental import pallas as pl
from jax.experimental.pallas import tpu as pltpu
from jax.sharding import PartitionSpec as P

MESH = pl.DeviceIdType.MESH
F32, BF16, I32 = jnp.float32, jnp.bfloat16, jnp.int32
K = 96
S = 192
T = 128
CH = 32
NCH = T // CH
PARTS = 3
UNITS = PARTS * NCH
ROWS = 3 * CH
MODE = 16
FORWARD, FINISH, COLLECT, ZLAG = 1, 2, 4, 2
MODE_A, MODE_B = 8, 11


def nn(a, b, precision=None):
    return lax.dot_general(a, b, (((1,), (0,)), ((), ())), preferred_element_type=F32, precision=precision)


def nt(a, b):
    return lax.dot_general(a, b, (((1,), (1,)), ((), ())), preferred_element_type=F32)


def pick(rows, columns, column_of, dtype=BF16):
    r = lax.broadcasted_iota(I32, (rows, columns), 0)
    return jnp.where(lax.broadcasted_iota(I32, (rows, columns), 1) == column_of(r), 1.0, 0.0).astype(dtype)


def main_kernel(
    field, core_x, core_y, core_z, x_second, x_third, y_first, y_third, z_first, z_second,
    out,
    own, par, wt, us, send, mid, ring, second, gath, hbuf, zrecv, fbuf, frecv,
    cx, cy, cz, tx2, tx3, ty1, ty3, tz1, tz2,
    czt, cxp, wy, zp, y1, x2, x3, g1, g2, g3, m12, arecv, msg, r1, r2,
    in_s, own_sem, par_s, par_r, mid_s, mid_r, dir_s, dir_r, com_s, com_r, sec_s, sec_r, z_s, z_r, f_s, f_r,
    ma_s, ma_r, mb_s, mb_r, mc_s, mc_r,
):
    t, g = lax.axis_index("xy"), lax.axis_index("gz")
    z, s = lax.div(t, 4), lax.rem(t, 4)
    xh, c = lax.div(s, 2), lax.rem(s, 2)
    xl, y = lax.div(g, 4), lax.rem(g, 4)
    X = xh * 2 + xl
    u, v = lax.div(t, 8), lax.rem(t, 8)
    mate = t + 1 - 2 * c

    def ring_dev(d, q):
        tt = t + (1 - d) * 2 * (lax.div(q, 2) - xh)
        gg = g + (1 - d) * 4 * (lax.rem(q, 2) - xl) + d * (q - y)
        return (tt, gg)

    def place(d):
        return (1 - d) * X + d * y

    def step(p, k):
        return lax.rem(p + k, 4)

    def copy(src, dst, ss, rs, dev):
        return pltpu.make_async_remote_copy(
            src_ref=src, dst_ref=dst, send_sem=ss, recv_sem=rs, device_id=dev, device_id_type=MESH
        )

    def own_copy(ch):
        return pltpu.make_async_copy(field.at[0, pl.ds(ch * CH, CH)], own.at[ch], own_sem.at[ch])

    def par_copy(ch):
        return copy(field.at[0, pl.ds(ch * CH, CH)], par.at[ch], par_s.at[ch], par_r.at[ch], (mate, g))

    def mid_copy(n, w):
        d = lax.rem(n, 2)
        p = place(d)
        src = send.at[n, pl.ds(step(p, 2) * 4 + 2 * w, 2)]
        return copy(src, mid.at[n, w], mid_s.at[n, w], mid_r.at[n, w], ring_dev(d, step(p, 1 + 2 * w)))

    def part(n, w, h):
        p = place(lax.rem(n, 2))
        return send.at[n, pl.ds(step(p, 1 + 2 * w) * 4 + 2 * h, 2)]

    def dir_copy(n, w):
        d = lax.rem(n, 2)
        dst = ring.at[n, w, pl.ds(2 * (1 - w), 2)]
        return copy(part(n, w, 1 - w), dst, dir_s.at[n, w], dir_r.at[n, w], ring_dev(d, step(place(d), 1 + 2 * w)))

    def com_copy(n, w):
        d = lax.rem(n, 2)
        dst = ring.at[n, w, pl.ds(2 * w, 2)]
        return copy(part(n, w, w), dst, com_s.at[n, w], com_r.at[n, w], ring_dev(d, step(place(d), 1 + 2 * w)))

    def sec_copy(n, k):
        d = lax.rem(n, 2)
        q = step(place(1 - d), k)
        src = send.at[n, place(d) * 4 + q]
        return copy(src, second.at[n, k - 1], sec_s.at[n, k - 1], sec_r.at[n, k - 1], ring_dev(1 - d, q))

    def z_copy(i, k):
        zz = lax.rem(z + k, 8)
        size = 128 if i == 1 else 96
        src, dst = hbuf.at[i, zz, pl.ds(0, size)], zrecv.at[i, k - 1, pl.ds(0, size)]
        return copy(src, dst, z_s.at[i, k - 1], z_r.at[i, k - 1], (zz * 4 + s, g))

    def f_copy(i, k):
        q = step(s, k)
        size = 4 if i == 1 else 3
        src, dst = fbuf.at[i, q, pl.ds(0, size)], frecv.at[i, k - 1, pl.ds(0, size)]
        return copy(src, dst, f_s.at[i, k - 1], f_r.at[i, k - 1], (z * 4 + q, g))

    def ma_copy(k):
        q = lax.rem(g + k, 8)
        return copy(m12.at[q], arecv.at[k - 1], ma_s.at[k - 1], ma_r.at[k - 1], (t, q))

    def mb_copy(k):
        q = lax.rem(v + k, 8)
        return copy(msg.at[q], r1.at[k - 1], mb_s.at[k - 1], mb_r.at[k - 1], (u * 8 + q, g))

    def mc_send(b):
        return copy(msg.at[8 + b], r2.at[u], mc_s.at[b], mc_r.at[u], (v * 4 + b, g))

    def mc_recv(k):
        return copy(msg.at[8], r2.at[k], mc_s.at[0], mc_r.at[k], (k * 8 + lax.div(t, 4), g))

    barrier = pltpu.get_barrier_semaphore()
    others = [ring_dev(0, step(X, 3 - 2 * xl))]
    others += [(z * 4 + step(s, k), g) for k in (1, 2, 3)]
    others += [(t, lax.rem(g + k, 8)) for k in range(1, 8)]
    others += [(lax.rem(z + k, 8) * 4 + s, g) for k in range(1, 8)]
    others += [((z + 1 - 2 * lax.rem(z, 2)) * 4 + step(s, k), g) for k in (1, 2, 3)]
    for dev in others:
        pl.semaphore_signal(barrier, inc=1, device_id=dev, device_id_type=MESH)
    for k in range(4):
        source = k * 8 + lax.div(t, 4)

        @pl.when(source != t)
        def _():
            pl.semaphore_signal(barrier, inc=1, device_id=(source, g), device_id_type=MESH)

    def columns(ref, base):
        return ref.at[:, pl.ds(pl.multiple_of(base, T), T)]

    loads = [
        (core_z, cz), (columns(core_y, v * T), cy.at[0]), (columns(core_y, (v + 1 - 2 * c) * T), cy.at[1]),
        (z_first, tz1), (z_second, tz2), (columns(y_first, v * T), ty1), (columns(y_third, v * T), ty3),
        (columns(x_second, u * T), tx2), (columns(x_third, u * T), tx3), (columns(core_x, u * T), cx),
    ]
    loads = [pltpu.make_async_copy(a, b, in_s.at[k]) for k, (a, b) in enumerate(loads)]
    for load in loads:
        load.start()

    def start_own(ch, _):
        own_copy(ch).start()
        return 0

    lax.fori_loop(0, NCH, start_own, 0)

    @pl.when(lax.div(t, 4) == v)
    def _():
        pl.semaphore_wait(barrier, len(others) + 3)

    @pl.when(lax.div(t, 4) != v)
    def _():
        pl.semaphore_wait(barrier, len(others) + 4)

    def start_par(ch, _):
        par_copy(ch).start()
        return 0

    lax.fori_loop(0, NCH, start_par, 0)
    for load in loads:
        load.wait()

    def r_of(row):
        h = jnp.where(row >= 48, 1, 0)
        rest = row - 48 * h
        e = rest & 15
        return 24 * (((e >> 2) & 1) * 4 + (e & 3)) + 12 * (e >> 3) + 6 * c + 3 * h + (rest >> 4)

    def eights(n):
        return lambda row: jnp.where((row & 7) < n, n * (row >> 3) + (row & 7), -1)

    eye = pick(T, T, lambda row: row)
    gap = jnp.zeros((32, T), BF16)
    czt[...] = nn(pick(96, S, r_of), cz[...]).astype(BF16)
    for o in range(2):
        low, high = cy[o, 0:128], cy[o, 128:192]
        wy[0, o * T : o * T + T, :] = nt(eye, jnp.concatenate([low, high, gap, gap], axis=0)).astype(BF16)
        wy[1, o * T : o * T + T, :] = nt(eye, jnp.concatenate([low, gap, gap, high], axis=0)).astype(BF16)
    zp[...] = nt(eye, jnp.concatenate([tz1[...], gap, tz2[...], gap], axis=0)).astype(BF16)
    y1[...] = nt(eye, jnp.concatenate([ty1[...], gap], axis=0))
    x2[...] = nt(eye, jnp.concatenate([tx2[...], gap], axis=0))
    turned = tx3[...].astype(F32)
    for n in range(T // MODE):
        x3[n, :, 0:MODE] = turned[:, n * MODE : n * MODE + MODE]
    cxp[...] = nn(pick(256, S, eights(6)), cx[...]).astype(BF16)
    g2[...] = jnp.zeros_like(g2)
    g3[...] = jnp.zeros_like(g3)

    def contract_z(ch):
        own_copy(ch).wait()
        par_copy(ch).wait_recv()
        for a in range(CH):
            both = jnp.concatenate([own[ch, a], par[ch, a]], axis=0)
            w = nt(czt[...], both).astype(BF16)
            for h in range(2):
                for i in range(PARTS):
                    at = (h * PARTS + i) * 16
                    wt[h, i, ch, a * 16 : a * 16 + 16, :] = w[at : at + 16]

    def contract_y(n):
        i, ch, d = lax.div(n, NCH), lax.rem(n, NCH), lax.rem(n, 2)
        for b in range(4):
            top = nn(wt[0, i, ch, b * 128 : b * 128 + 128, :], wy[0])
            bot = nn(wt[1, i, ch, b * 128 : b * 128 + 128, :], wy[1])
            rest = top[:, 128:] + bot[:, 128:]
            for a in range(8):
                at, lo = (b * 8 + a) * 48, a * 16
                us[at : at + 16, :] = top[lo : lo + 16, 0:128]
                us[at + 16 : at + 32, :] = bot[lo : lo + 16, 0:128]
                us[at + 32 : at + 48, :] = rest[lo : lo + 16]
        for e in range(16):
            q = (1 - d) * e + d * ((e % 4) * 4 + e // 4)
            for kind in range(3):
                block = us[pl.ds(kind * 16 + e, CH, stride=48), :]
                send[n, q, kind * CH : kind * CH + CH, :] = block.astype(BF16)
        for w in range(2):
            mid_copy(n, w).start()
        for w in range(2):
            dir_copy(n, w).start()

    def modes(n):
        ch, off = lax.div(n, 2), lax.rem(n, 2) * MODE
        rows = x2[pl.ds(pl.multiple_of(n * MODE, MODE), MODE), :]
        total = g2[...]
        factors = []
        for a in range(MODE):
            m = nn(own[ch, off + a], zp[...])
            g1[pl.ds(n * MODE + a, 1), :] = jnp.sum(m[:, 0:128] * y1[...], axis=0, keepdims=True)
            total = total + m[:, 128:] * rows[a : a + 1]
            factors.append((ty3[...].astype(F32) * x3[n, :, a : a + 1]).astype(BF16))
        g2[...] = total
        block = own[ch, pl.ds(off, MODE)].reshape(MODE * T, T)
        g3[...] += nn(jnp.concatenate(factors, axis=1), block)

    def forward(n):
        p = place(lax.rem(n, 2))
        for w in range(2):
            mid_copy(n, w).wait_recv()
            base = step(p, 1 + 2 * w) * 4 + 2 * w
            for h in range(2):
                mine = send[n, base + h].astype(F32)
                send[n, base + h] = (mine + mid[n, w, h].astype(F32)).astype(BF16)
            com_copy(n, w).start()

    def finish(n):
        p = place(lax.rem(n, 2))
        for w in range(2):
            dir_copy(n, w).wait_recv()
            com_copy(n, w).wait_recv()
        for b in range(4):
            tot = send[n, p * 4 + b].astype(F32) + ring[n, 0, b].astype(F32) + ring[n, 1, b].astype(F32)
            send[n, p * 4 + b] = tot.astype(BF16)
        for k in (1, 2, 3):
            sec_copy(n, k).start()

    def collect(n):
        i, ch, d = lax.div(n, NCH), lax.rem(n, NCH), lax.rem(n, 2)
        for k in (1, 2, 3):
            sec_copy(n, k).wait_recv()
        tot = send[n, place(d) * 4 + place(1 - d)].astype(F32)
        for k in range(3):
            tot = tot + second[n, k].astype(F32)
        tot = tot.astype(BF16)
        for kind in range(3):
            gath[i, kind, pl.ds(pl.multiple_of(ch * CH, CH), CH), :] = tot[kind * CH : kind * CH + CH]

    def contract_x(i):
        for kind in range(3):
            piece = nn(cxp[...], gath[i, kind])
            hbuf[i, :, kind * 32 : kind * 32 + 32, :] = piece.astype(BF16).reshape(8, 32, T)
        if i == 1:
            piece = nn(pick(256, K, eights(3)), g3[...].astype(BF16))
            hbuf[i, :, 96:128, :] = piece.astype(BF16).reshape(8, 32, T)
        for k in (4, 3, 5, 2, 6, 1, 7):
            z_copy(i, k).start()

    def finish_z(i):
        for k in range(1, 8):
            z_copy(i, k).wait_recv()
        for kind in range(4 if i == 1 else 3):
            at = kind * 32
            tot = hbuf[i, z, at : at + 32, :].astype(F32)
            for k in range(7):
                tot = tot + zrecv[i, k, at : at + 32, :].astype(F32)
            fbuf[i, :, kind] = tot.reshape(4, 8, T)
        for k in (1, 2, 3):
            f_copy(i, k).start()

    def modes_a():
        high = lax.Precision.HIGHEST
        one = nn(pick(T, T, lambda q: 16 * ((q >> 1) & 7) + 2 * (q >> 4) + (q & 1), F32), g1[...], high)
        two = nn(pick(T, T, lambda q: 32 * ((q >> 2) & 3) + 4 * (q >> 4) + (q & 3), F32), g2[...], high)
        m12[:, 0:16, :] = one.reshape(8, 16, T)
        m12[:, 16:32, :] = two.reshape(8, 16, T)
        for k in range(1, 8):
            ma_copy(k).start()

    def modes_b():
        total = m12[g]
        for k in range(1, 8):
            ma_copy(k).wait_recv()
            total = total + arecv[k - 1]

        def source_row(q):
            i = q & 7
            low = jnp.where(i < 2, 2 * (q >> 3) + i, -1)
            return jnp.where(q < 64, low, jnp.where(i < 4, 16 + 4 * ((q - 64) >> 3) + i, -1))

        msg[...] = nn(pick(96, 32, source_row, F32), total, lax.Precision.HIGHEST).reshape(12, 8, T)
        for k in range(1, 8):
            mb_copy(k).start()
        for b in range(4):

            @pl.when(v * 4 + b != t)
            def _():
                mc_send(b).start()

            @pl.when(v * 4 + b == t)
            def _():
                r2[u] = msg[8 + b]

    def turn(n, _):
        @pl.when(n < NCH)
        def _():
            contract_z(n)

        @pl.when(n < UNITS)
        def _():
            contract_y(n)

        @pl.when((n >= FORWARD) & (n < UNITS + FORWARD))
        def _():
            forward(n - FORWARD)

        @pl.when(n < T // MODE)
        def _():
            modes(n)

        @pl.when((n >= FINISH) & (n < UNITS + FINISH))
        def _():
            finish(n - FINISH)

        @pl.when((n >= COLLECT) & (n < UNITS + COLLECT))
        def _():
            collect(n - COLLECT)

        for i in range(PARTS):
            last = NCH * i + NCH - 1 + COLLECT

            @pl.when(n == last)
            def _():
                contract_x(i)

            @pl.when(n == last + ZLAG)
            def _():
                finish_z(i)

        @pl.when(n == MODE_A)
        def _():
            modes_a()

        @pl.when(n == MODE_B)
        def _():
            modes_b()

        return 0

    lax.fori_loop(0, UNITS + COLLECT + ZLAG, turn, 0)

    first = msg[v]
    for k in range(1, 8):
        mb_copy(k).wait_recv()
        first = first + r1[k - 1]
    out[37] = first
    for k in range(4):

        @pl.when(k * 8 + lax.div(t, 4) != t)
        def _():
            mc_recv(k).wait_recv()

    out[38] = r2[0] + r2[1] + r2[2] + r2[3]
    third = fbuf[1, s, 3]
    for i in range(PARTS):
        for kind in range(3):
            out[s * 9 + kind * 3 + i] = fbuf[i, s, kind]
        for k in (1, 2, 3):
            f_copy(i, k).wait_recv()
            for kind in range(3):
                out[step(s, 4 - k) * 9 + kind * 3 + i] = frecv[i, k - 1, kind]
            if i == 1:
                third = third + frecv[1, k - 1, 3]
    out[36] = third

    def drain(n, _):
        for w in range(2):
            mid_copy(n, w).wait_send()
            dir_copy(n, w).wait_send()
            com_copy(n, w).wait_send()
        for k in (1, 2, 3):
            sec_copy(n, k).wait_send()
        return 0

    lax.fori_loop(0, UNITS, drain, 0)
    for ch in range(NCH):
        par_copy(ch).wait_send()
    for i in range(PARTS):
        for k in range(1, 8):
            z_copy(i, k).wait_send()
        for k in (1, 2, 3):
            f_copy(i, k).wait_send()
    for k in range(1, 8):
        ma_copy(k).wait_send()
        mb_copy(k).wait_send()
    for b in range(4):

        @pl.when(v * 4 + b != t)
        def _():
            mc_send(b).wait_send()


def outputs_kernel(x, one, two, three, core):
    one[...] = x[37 * 8 : 37 * 8 + 2, 0:K]
    two[...] = x[38 * 8 : 38 * 8 + 4, 0:K]
    three[...] = x[36 * 8 : 36 * 8 + 3, :]
    for p in range(6):
        rows = x[pl.ds(p, 36, stride=8), :]
        for q in range(4):
            core[p, 6 * q : 6 * q + 6, 0:128] = rows[9 * q : 9 * q + 6]
            core[p, 6 * q : 6 * q + 3, 128:192] = rows[9 * q + 6 : 9 * q + 9, 0:64]
            core[p, 6 * q + 3 : 6 * q + 6, 128:192] = rows[9 * q + 6 : 9 * q + 9, 64:128]


def shards(field, *small):
    vm, hbm = pl.BlockSpec(memory_space=pltpu.VMEM), pl.BlockSpec(memory_space=pl.ANY)
    dma, mem = pltpu.SemaphoreType.DMA, pltpu.VMEM
    unit = [dma((UNITS, 2))] * 6 + [dma((UNITS, 3))] * 2
    raw = pl.pallas_call(
        main_kernel,
        out_shape=jax.ShapeDtypeStruct((39, 8, 128), F32),
        in_specs=[hbm] * 10,
        out_specs=vm,
        scratch_shapes=[
            mem((NCH, CH, T, T), BF16),
            mem((NCH, CH, T, T), BF16),
            mem((2, PARTS, NCH, CH * 16, 256), BF16),
            mem((CH * 48, 128), F32),
            mem((UNITS, 16, ROWS, 128), BF16),
            mem((UNITS, 2, 2, ROWS, 128), BF16),
            mem((UNITS, 2, 4, ROWS, 128), BF16),
            mem((UNITS, 3, ROWS, 128), BF16),
            mem((PARTS, 3, T, 128), BF16),
            mem((PARTS, 8, 128, 128), BF16),
            mem((PARTS, 7, 128, 128), BF16),
            mem((PARTS, 4, 4, 8, 128), F32),
            mem((PARTS, 3, 4, 8, 128), F32),
            mem((S, T), BF16), mem((2, S, T), BF16), mem((S, T), BF16),
            mem((K, T), BF16), mem((K, T), BF16), mem((K, T), BF16), mem((K, T), BF16),
            mem((K, T), BF16), mem((K, T), BF16),
            mem((K, T), BF16),
            mem((256, T), BF16),
            mem((2, 2 * T, 256), BF16),
            mem((T, 256), BF16),
            mem((T, 128), F32), mem((T, 128), F32),
            mem((T // MODE, K, 128), F32),
            mem((T, 128), F32), mem((T, 128), F32), mem((K, T), F32),
            mem((8, 32, 128), F32), mem((7, 32, 128), F32),
            mem((12, 8, 128), F32), mem((7, 8, 128), F32), mem((4, 8, 128), F32),
            dma((10,)), dma((NCH,)), dma((NCH,)), dma((NCH,)),
            *unit,
            dma((PARTS, 7)), dma((PARTS, 7)), dma((PARTS, 3)), dma((PARTS, 3)),
            dma((7,)), dma((7,)), dma((7,)), dma((7,)), dma((4,)), dma((4,)),
        ],
        compiler_params=pltpu.CompilerParams(
            collective_id=0, has_side_effects=True, vmem_limit_bytes=56 * 1024 * 1024
        ),
    )(field, *[x.T for x in small])
    one, two, three, core = pl.pallas_call(
        outputs_kernel,
        out_shape=(
            jax.ShapeDtypeStruct((2, K), F32),
            jax.ShapeDtypeStruct((4, K), F32),
            jax.ShapeDtypeStruct((3, T), F32),
            jax.ShapeDtypeStruct((6, 24, S), F32),
        ),
        in_specs=[vm],
        out_specs=(vm, vm, vm, vm),
    )(raw.reshape(39 * 8, 128))
    return (one, two, three, core.transpose(0, 2, 1))


def solution(mesh):
    return jax.shard_map(
        shards,
        mesh=mesh,
        in_specs=(
            P("xy", None, None, "gz"),
            P(), P(), P("gz", None), P(), P(), P(), P(), P("gz", None), P("gz", None),
        ),
        out_specs=(
            P(("xy", "gz"), None),
            P(("xy", "gz"), None),
            P("xy", "gz"),
            P("xy", None, "gz"),
        ),
        check_vma=False,
    )
```

time: 420 us -> 74.8 us (0.18); the launches traced: 416 us -> 74.7 us
  waiting for transfers between devices: 224 us -> 0 us
  blocking collectives: 127 us -> 0 us
  Pallas kernels: 0 us -> 74 us
  matrix products: 36.6 us -> 0 us
  between operations: 16.3 us -> 0.64 us
  other arithmetic: 6.47 us -> 0 us
  local copies, waits for them, and re-layouts: 4.9 us -> 0 us
    reduce_scatter x2 -> x0, waiting for transfers between devices: 224 us -> none  [the longest x1 224 us: shards(): lax.psum_scatter(jnp.einsum('pbz,bq->pqz', lowered, y_rows, preferred_ele...]
    unnamed x1 -> x0, blocking collectives: 127 us -> none
    pallas_call x0 -> x2, Pallas kernels: none -> 74 us  [the longest x1 72.3 us: shards(): pl.pallas_call(main_kernel, out_shape=jax.ShapeDtypeStruct((39, 8, 128),...]
    dot_general x5 -> x0, matrix products: 36.6 us -> none  [the longest x1 17.9 us: shards(): jnp.einsum('pbz,bq->pqz', lowered, y_rows, preferred_element_type=jnp.flo...]
    unnamed x18 -> x0, local copies, waits for them, and re-layouts: 4.56 us -> none
    reduce_sum x1 -> x0, other arithmetic: 4.22 us -> none  [shards(): jnp.sum(paired[:, :, K:] * row_slice(x_second, x_offset, TX).astype(jnp.f...]
  transfers between devices with their start and end apart: 3 -> 0, of which waited for: 1 -> 0; matrix products, arithmetic and copies ran while one was open for 6% -> 0% of each run, Pallas kernels for 0% -> 0%
where the time goes in v2:
time: 74.8 us; the launch traced here: 74.7 us
  Pallas kernels  74 us (99%)
    pallas_call x1, Pallas kernels, shards(): pl.pallas_call(main_kernel, out_shape=jax.ShapeDtypeStruct((39, 8, 128),...  72.3 us
    pallas_call x1, Pallas kernels, shards(): pl.pallas_call(outputs_kernel, out_shape=(jax.ShapeDtypeStruct((2, K), F3...  1.68 us

profile of v2, /device:TPU:1, one launch (start us, length us, event | category | flops | bytes accessed | tf_op | source)
XLA Modules:
  0.0 74.7 jit_solution(9651753308400990341)
XLA Ops:
  0.6 72.3 %shard_map.129 = f32[39,8,128]{2,1,0:T(8,128)} custom-call(bf16[1,128,128,128]{3,2,1,0:T(8,128)(2,1)} %field.1, bf16[192,512]{1,0:T(8,128)(2,1)} %bitcast.13, bf16[192,1024]{1,0:T(8,128)(2,1)} %bitcast.12, bf16[192,128]{1,0:T(8,128)(2,1)} %bitcast.18, bf16[96,512]{1,0:T(8,128)(2,1)} %bitcast.16, bf16[96,512]{1,0:T(8,128)(2,1)} %bitcast.17, ...), custom_call_target="tpu_custom_call" | custom-call | tf_op jit(solution)/shard_map/pallas_call | solution.py:450
  73.0 1.7 %shard_map.130 = (f32[2,96]{1,0:T(2,128)}, f32[4,96]{1,0:T(4,128)}, f32[3,128]{1,0:T(4,128)}, f32[6,24,192]{2,1,0:T(8,128)}) custom-call(f32[312,128]{1,0:T(8,128)} %bitcast.11), custom_call_target="tpu_custom_call" | custom-call | tf_op jit(solution)/shard_map/pallas_call | solution.py:490

commit v3 on v2

--- a/solution.py
+++ b/solution.py
@@ -16,8 +16,8 @@
 UNITS = PARTS * NCH
 ROWS = 3 * CH
 MODE = 16
-FORWARD, FINISH, COLLECT, ZLAG = 1, 2, 4, 2
-MODE_A, MODE_B = 8, 11
+DIRECT, FORWARD, FINISH, COLLECT, ZLAG = 1, 2, 5, 8, 6
+MODE_0, MODE_A, MODE_B = 4, 12, 16
 
 
 def nn(a, b, precision=None):
@@ -70,7 +70,7 @@
         return pltpu.make_async_copy(field.at[0, pl.ds(ch * CH, CH)], own.at[ch], own_sem.at[ch])
 
     def par_copy(ch):
-        return copy(field.at[0, pl.ds(ch * CH, CH)], par.at[ch], par_s.at[ch], par_r.at[ch], (mate, g))
+        return copy(own.at[ch], par.at[ch], par_s.at[ch], par_r.at[ch], (mate, g))
 
     def mid_copy(n, w):
         d = lax.rem(n, 2)
@@ -165,11 +165,8 @@
     def _():
         pl.semaphore_wait(barrier, len(others) + 4)
 
-    def start_par(ch, _):
-        par_copy(ch).start()
-        return 0
-
-    lax.fori_loop(0, NCH, start_par, 0)
+    own_copy(0).wait()
+    par_copy(0).start()
     for load in loads:
         load.wait()
 
@@ -199,9 +196,19 @@
     g2[...] = jnp.zeros_like(g2)
     g3[...] = jnp.zeros_like(g3)
 
+    def start_par(ch):
+        own_copy(ch).wait()
+        par_copy(ch).start()
+
+    start_par(1)
+
     def contract_z(ch):
-        own_copy(ch).wait()
         par_copy(ch).wait_recv()
+
+        @pl.when(ch < NCH - 2)
+        def _():
+            start_par(ch + 2)
+
         for a in range(CH):
             both = jnp.concatenate([own[ch, a], par[ch, a]], axis=0)
             w = nt(czt[...], both).astype(BF16)
@@ -228,8 +235,6 @@
                 send[n, q, kind * CH : kind * CH + CH, :] = block.astype(BF16)
         for w in range(2):
             mid_copy(n, w).start()
-        for w in range(2):
-            dir_copy(n, w).start()
 
     def modes(n):
         ch, off = lax.div(n, 2), lax.rem(n, 2) * MODE
@@ -341,13 +346,18 @@
         def _():
             contract_y(n)
 
+        @pl.when((n >= DIRECT) & (n < UNITS + DIRECT))
+        def _():
+            for w in range(2):
+                dir_copy(n - DIRECT, w).start()
+
         @pl.when((n >= FORWARD) & (n < UNITS + FORWARD))
         def _():
             forward(n - FORWARD)
 
-        @pl.when(n < T // MODE)
-        def _():
-            modes(n)
+        @pl.when((n >= MODE_0) & (n < MODE_0 + T // MODE))
+        def _():
+            modes(n - MODE_0)
 
         @pl.when((n >= FINISH) & (n < UNITS + FINISH))
         def _():

time: 74.8 us -> 65 us (0.87)
  Pallas kernels: 74 us -> 64.2 us
    pallas_call x1, Pallas kernels: 72.3 us -> 62.5 us  [shards(): pl.pallas_call(main_kernel, out_shape=jax.ShapeDtypeStruct((39, 8, 128),...]
where the time goes in v3:
time: 65 us; the launch traced here: 64.9 us
  Pallas kernels  64.2 us (99%)
    pallas_call x1, Pallas kernels, shards(): pl.pallas_call(main_kernel, out_shape=jax.ShapeDtypeStruct((39, 8, 128),...  62.5 us
    pallas_call x1, Pallas kernels, shards(): pl.pallas_call(outputs_kernel, out_shape=(jax.ShapeDtypeStruct((2, K), F3...  1.68 us

profile of v3, /device:TPU:1, one launch (start us, length us, event | category | flops | bytes accessed | tf_op | source)
XLA Modules:
  0.0 64.9 jit_solution(662858904850116436)
XLA Ops:
  0.6 62.5 %shard_map.129 = f32[39,8,128]{2,1,0:T(8,128)} custom-call(bf16[1,128,128,128]{3,2,1,0:T(8,128)(2,1)} %field.1, bf16[192,512]{1,0:T(8,128)(2,1)} %bitcast.13, bf16[192,1024]{1,0:T(8,128)(2,1)} %bitcast.12, bf16[192,128]{1,0:T(8,128)(2,1)} %bitcast.18, bf16[96,512]{1,0:T(8,128)(2,1)} %bitcast.16, bf16[96,512]{1,0:T(8,128)(2,1)} %bitcast.17, ...), custom_call_target="tpu_custom_call" | custom-call | tf_op jit(solution)/shard_map/pallas_call | solution.py:460
  63.2 1.7 %shard_map.130 = (f32[2,96]{1,0:T(2,128)}, f32[4,96]{1,0:T(4,128)}, f32[3,128]{1,0:T(4,128)}, f32[6,24,192]{2,1,0:T(8,128)}) custom-call(f32[312,128]{1,0:T(8,128)} %bitcast.11), custom_call_target="tpu_custom_call" | custom-call | tf_op jit(solution)/shard_map/pallas_call | solution.py:500

commit v4 on v3

v4 whole, which is shorter than its diff:
```python
import jax
import jax.numpy as jnp
from jax import lax
from jax.experimental import pallas as pl
from jax.experimental.pallas import tpu as pltpu
from jax.sharding import PartitionSpec as P

MESH = pl.DeviceIdType.MESH
F32, BF16, I32 = jnp.float32, jnp.bfloat16, jnp.int32
K = 96
S = 192
T = 128
CH = 32
NCH = T // CH
PIECES = (((0, 0), (1, 0), (2, 0)), ((0, 1), (1, 1), (2, 1)), ((0, 2), (1, 2), (2, 2)))
THIRD = 1
PARTS = len(PIECES)
UNITS = PARTS * NCH
MOST = 3
ROWS = MOST * CH
MODE = 16
DIRECT, FORWARD, FINISH, COLLECT, ZLAG = 1, 2, 5, 8, 6
MODE_0, MODE_A, MODE_B = 4, 12, 16


def nn(a, b, precision=None):
    return lax.dot_general(a, b, (((1,), (0,)), ((), ())), preferred_element_type=F32, precision=precision)


def nt(a, b):
    return lax.dot_general(a, b, (((1,), (1,)), ((), ())), preferred_element_type=F32)


def pick(rows, columns, column_of, dtype=BF16):
    r = lax.broadcasted_iota(I32, (rows, columns), 0)
    return jnp.where(lax.broadcasted_iota(I32, (rows, columns), 1) == column_of(r), 1.0, 0.0).astype(dtype)


def main_kernel(
    field, core_x, core_y, core_z, x_second, x_third, y_first, y_third, z_first, z_second,
    out,
    own, par, wt, us, send, mid, ring, second, gath, hbuf, zrecv, fbuf, frecv,
    cx, cy, cz, tx2, tx3, ty1, ty3, tz1, tz2,
    czt, cxp, wy, zp, y1, x2, x3, g1, g2, g3, m12, arecv, msg, r1, r2,
    in_s, own_sem, par_s, par_r, mid_s, mid_r, dir_s, dir_r, com_s, com_r, sec_s, sec_r, z_s, z_r, f_s, f_r,
    ma_s, ma_r, mb_s, mb_r, mc_s, mc_r,
):
    t, g = lax.axis_index("xy"), lax.axis_index("gz")
    z, s = lax.div(t, 4), lax.rem(t, 4)
    xh, c = lax.div(s, 2), lax.rem(s, 2)
    xl, y = lax.div(g, 4), lax.rem(g, 4)
    X = xh * 2 + xl
    u, v = lax.div(t, 8), lax.rem(t, 8)
    mate = t + 1 - 2 * c

    def ring_dev(d, q):
        tt = t + (1 - d) * 2 * (lax.div(q, 2) - xh)
        gg = g + (1 - d) * 4 * (lax.rem(q, 2) - xl) + d * (q - y)
        return (tt, gg)

    def place(d):
        return (1 - d) * X + d * y

    def step(p, k):
        return lax.rem(p + k, 4)

    def copy(src, dst, ss, rs, dev):
        return pltpu.make_async_remote_copy(
            src_ref=src, dst_ref=dst, send_sem=ss, recv_sem=rs, device_id=dev, device_id_type=MESH
        )

    def own_copy(ch):
        return pltpu.make_async_copy(field.at[0, pl.ds(ch * CH, CH)], own.at[ch], own_sem.at[ch])

    def par_copy(ch):
        return copy(field.at[0, pl.ds(ch * CH, CH)], par.at[ch], par_s.at[ch], par_r.at[ch], (mate, g))

    def block(n, place_of, size):
        return send.at[n, place_of, pl.ds(0, size)]

    def mid_copy(n, w, size):
        d = lax.rem(n, 2)
        p = place(d)
        src, dst = block(n, pl.ds(step(p, 2) * 4 + 2 * w, 2), size), mid.at[n, pl.ds(2 * w, 2), pl.ds(0, size)]
        return copy(src, dst, mid_s.at[n, w], mid_r.at[n, w], ring_dev(d, step(p, 1 + 2 * w)))

    def opp_copy(n, size):
        d = lax.rem(n, 2)
        q = step(place(d), 2)
        src, dst = block(n, pl.ds(q * 4, 4), size), mid.at[n, pl.ds(0, 4), pl.ds(0, size)]
        return copy(src, dst, mid_s.at[n, 0], mid_r.at[n, 0], ring_dev(d, q))

    def near_copy(n, w, h, count, size, ss, rs):
        d = lax.rem(n, 2)
        q = step(place(d), 1 + 2 * w)
        src, dst = block(n, pl.ds(q * 4 + h, count), size), ring.at[n, w, pl.ds(h, count), pl.ds(0, size)]
        return copy(src, dst, ss.at[n, w], rs.at[n, w], ring_dev(d, q))

    def dir_copy(n, w, size):
        return near_copy(n, w, 2 * (1 - w), 2, size, dir_s, dir_r)

    def com_copy(n, w, size):
        return near_copy(n, w, 2 * w, 2, size, com_s, com_r)

    def all_copy(n, w, size):
        return near_copy(n, w, 0, 4, size, dir_s, dir_r)

    def sec_copy(n, k, size):
        d = lax.rem(n, 2)
        q = step(place(1 - d), k)
        src, dst = block(n, place(d) * 4 + q, size), second.at[n, k - 1, pl.ds(0, size)]
        return copy(src, dst, sec_s.at[n, k - 1], sec_r.at[n, k - 1], ring_dev(1 - d, q))

    def slabs(i):
        return len(PIECES[i]) + (i == THIRD)

    def lines(i):
        used = 24 * len(PIECES[i]) + (12 if i == THIRD else 0)
        return (used + 15) // 16 * 16

    def z_copy(i, k):
        zz = lax.rem(z + k, 8)
        size = lines(i)
        src, dst = hbuf.at[i, zz, pl.ds(0, size)], zrecv.at[i, k - 1, pl.ds(0, size)]
        return copy(src, dst, z_s.at[i, k - 1], z_r.at[i, k - 1], (zz * 4 + s, g))

    def f_copy(i, k):
        q = step(s, k)
        size = slabs(i)
        src, dst = fbuf.at[i, q, pl.ds(0, size)], frecv.at[i, k - 1, pl.ds(0, size)]
        return copy(src, dst, f_s.at[i, k - 1], f_r.at[i, k - 1], (z * 4 + q, g))

    def ma_copy(k):
        q = lax.rem(g + k, 8)
        return copy(m12.at[q], arecv.at[k - 1], ma_s.at[k - 1], ma_r.at[k - 1], (t, q))

    def mb_copy(k):
        q = lax.rem(v + k, 8)
        return copy(msg.at[q], r1.at[k - 1], mb_s.at[k - 1], mb_r.at[k - 1], (u * 8 + q, g))

    def mc_send(b):
        return copy(msg.at[8 + b], r2.at[u], mc_s.at[b], mc_r.at[u], (v * 4 + b, g))

    def mc_recv(k):
        return copy(msg.at[8], r2.at[k], mc_s.at[0], mc_r.at[k], (k * 8 + lax.div(t, 4), g))

    barrier = pltpu.get_barrier_semaphore()
    others = [ring_dev(0, step(X, 3 - 2 * xl))]
    others += [(z * 4 + step(s, k), g) for k in (1, 2, 3)]
    others += [(t, lax.rem(g + k, 8)) for k in range(1, 8)]
    others += [(lax.rem(z + k, 8) * 4 + s, g) for k in range(1, 8)]
    others += [((z + 1 - 2 * lax.rem(z, 2)) * 4 + step(s, k), g) for k in (1, 2, 3)]
    for dev in others:
        pl.semaphore_signal(barrier, inc=1, device_id=dev, device_id_type=MESH)
    for k in range(4):
        source = k * 8 + lax.div(t, 4)

        @pl.when(source != t)
        def _():
            pl.semaphore_signal(barrier, inc=1, device_id=(source, g), device_id_type=MESH)

    def columns(ref, base):
        return ref.at[:, pl.ds(pl.multiple_of(base, T), T)]

    loads = [
        (core_z, cz), (columns(core_y, v * T), cy.at[0]), (columns(core_y, (v + 1 - 2 * c) * T), cy.at[1]),
        (z_first, tz1), (z_second, tz2), (columns(y_first, v * T), ty1), (columns(y_third, v * T), ty3),
        (columns(x_second, u * T), tx2), (columns(x_third, u * T), tx3), (columns(core_x, u * T), cx),
    ]
    loads = [pltpu.make_async_copy(a, b, in_s.at[k]) for k, (a, b) in enumerate(loads)]
    own_copy(0).start()
    for load in loads:
        load.start()

    def start_own(ch, _):
        own_copy(ch).start()
        return 0

    lax.fori_loop(1, NCH, start_own, 0)

    @pl.when(lax.div(t, 4) == v)
    def _():
        pl.semaphore_wait(barrier, len(others) + 3)

    @pl.when(lax.div(t, 4) != v)
    def _():
        pl.semaphore_wait(barrier, len(others) + 4)

    par_copy(0).start()
    for load in loads[0:3]:
        load.wait()

    def r_of(row):
        h = jnp.where(row >= 48, 1, 0)
        rest = row - 48 * h
        e = rest & 15
        return 24 * (((e >> 2) & 1) * 4 + (e & 3)) + 12 * (e >> 3) + 6 * c + 3 * h + (rest >> 4)

    eye = pick(T, T, lambda row: row)
    gap = jnp.zeros((32, T), BF16)
    czt[...] = nn(pick(96, S, r_of), cz[...]).astype(BF16)
    for o in range(2):
        low, high = cy[o, 0:128], cy[o, 128:192]
        wy[0, o * T : o * T + T, :] = nt(eye, jnp.concatenate([low, high, gap, gap], axis=0)).astype(BF16)
        wy[1, o * T : o * T + T, :] = nt(eye, jnp.concatenate([low, gap, gap, high], axis=0)).astype(BF16)
    par_copy(1).start()

    def prepare():
        for load in loads[3:]:
            load.wait()
        zp[...] = nt(eye, jnp.concatenate([tz1[...], gap, tz2[...], gap], axis=0)).astype(BF16)
        y1[...] = nt(eye, jnp.concatenate([ty1[...], gap], axis=0))
        x2[...] = nt(eye, jnp.concatenate([tx2[...], gap], axis=0))
        turned = tx3[...].astype(F32)
        for n in range(T // MODE):
            x3[n, :, 0:MODE] = turned[:, n * MODE : n * MODE + MODE]
        cxp[...] = cx[...]
        fbuf[...] = jnp.zeros_like(fbuf)
        g2[...] = jnp.zeros_like(g2)
        g3[...] = jnp.zeros_like(g3)

    def contract_z(ch):
        own_copy(ch).wait()
        par_copy(ch).wait_recv()

        @pl.when(ch < NCH - 2)
        def _():
            par_copy(ch + 2).start()

        for a in range(CH):
            both = jnp.concatenate([own[ch, a], par[ch, a]], axis=0)
            w = nt(czt[...], both).astype(BF16)
            for h in range(2):
                for i in range(3):
                    at = (h * 3 + i) * 16
                    wt[h, i, ch, a * 16 : a * 16 + 16, :] = w[at : at + 16]

    def contract_y(n, k):
        ch, d, count = lax.rem(n, NCH), lax.rem(n, 2), len(PIECES[k])
        for b in range(CH // 8):
            made = {}
            for i in range(3):
                kinds = [kind for kind, index in PIECES[k] if index == i]
                if kinds:
                    first = wt[0, i, ch, b * 128 : b * 128 + 128, :]
                    other = wt[1, i, ch, b * 128 : b * 128 + 128, :]
                if kinds == [0, 1, 2]:
                    top, bot = nn(first, wy[0]), nn(other, wy[1])
                    made[0, i], made[1, i], made[2, i] = top[:, 0:128], bot[:, 0:128], top[:, 128:] + bot[:, 128:]
                elif kinds == [0, 1]:
                    made[0, i], made[1, i] = nn(first, wy[0, :, 0:128]), nn(other, wy[1, :, 0:128])
                elif kinds == [2]:
                    made[2, i] = nn(first, wy[0, :, 128:]) + nn(other, wy[1, :, 128:])
            for a in range(8):
                for m, piece in enumerate(PIECES[k]):
                    at = ((b * 8 + a) * count + m) * 16
                    us[at : at + 16, :] = made[piece][a * 16 : a * 16 + 16]
        for e in range(16):
            q = (1 - d) * e + d * ((e % 4) * 4 + e // 4)
            for m in range(count):
                lines = us[pl.ds(m * 16 + e, CH, stride=16 * count), :]
                send[n, q, m * CH : m * CH + CH, :] = lines.astype(BF16)
        if count == 1:
            opp_copy(n, CH).start()
            for w in range(2):
                all_copy(n, w, CH).start()
        else:
            for w in range(2):
                mid_copy(n, w, count * CH).start()

    def direct(n, k):
        if len(PIECES[k]) > 1:
            for w in range(2):
                dir_copy(n, w, len(PIECES[k]) * CH).start()

    def modes(n):
        ch, off = lax.div(n, 2), lax.rem(n, 2) * MODE
        rows = x2[pl.ds(pl.multiple_of(n * MODE, MODE), MODE), :]
        total = g2[...]
        factors = []
        for a in range(MODE):
            m = nn(own[ch, off + a], zp[...])
            g1[pl.ds(n * MODE + a, 1), :] = jnp.sum(m[:, 0:128] * y1[...], axis=0, keepdims=True)
            total = total + m[:, 128:] * rows[a : a + 1]
            factors.append((ty3[...].astype(F32) * x3[n, :, a : a + 1]).astype(BF16))
        g2[...] = total
        block = own[ch, pl.ds(off, MODE)].reshape(MODE * T, T)
        g3[...] += nn(jnp.concatenate(factors, axis=1), block)

    def forward(n, k):
        p, size = place(lax.rem(n, 2)), len(PIECES[k]) * CH
        if len(PIECES[k]) > 1:
            for w in range(2):
                mid_copy(n, w, size).wait_recv()
                base = step(p, 1 + 2 * w) * 4 + 2 * w
                for h in range(2):
                    mine = send[n, base + h, 0:size].astype(F32)
                    send[n, base + h, 0:size] = (mine + mid[n, 2 * w + h, 0:size].astype(F32)).astype(BF16)
                com_copy(n, w, size).start()

    def finish(n, k):
        p, size = place(lax.rem(n, 2)), len(PIECES[k]) * CH
        if len(PIECES[k]) > 1:
            for w in range(2):
                dir_copy(n, w, size).wait_recv()
                com_copy(n, w, size).wait_recv()
        else:
            opp_copy(n, size).wait_recv()
            for w in range(2):
                all_copy(n, w, size).wait_recv()
        for b in range(4):
            tot = send[n, p * 4 + b, 0:size].astype(F32) + ring[n, 0, b, 0:size].astype(F32)
            tot = tot + ring[n, 1, b, 0:size].astype(F32)
            if len(PIECES[k]) == 1:
                tot = tot + mid[n, b, 0:size].astype(F32)
            send[n, p * 4 + b, 0:size] = tot.astype(BF16)
        for o in (1, 2, 3):
            sec_copy(n, o, size).start()

    def collect(n, k):
        ch, d, size = lax.rem(n, NCH), lax.rem(n, 2), len(PIECES[k]) * CH
        for o in (1, 2, 3):
            sec_copy(n, o, size).wait_recv()
        tot = send[n, place(d) * 4 + place(1 - d), 0:size].astype(F32)
        for o in range(3):
            tot = tot + second[n, o, 0:size].astype(F32)
        tot = tot.astype(BF16)
        for m in range(len(PIECES[k])):
            gath[k, m, pl.ds(pl.multiple_of(ch * CH, CH), CH), :] = tot[m * CH : m * CH + CH]

    def drain(n, k):
        size = len(PIECES[k]) * CH
        if len(PIECES[k]) > 1:
            for w in range(2):
                mid_copy(n, w, size).wait_send()
                dir_copy(n, w, size).wait_send()
                com_copy(n, w, size).wait_send()
        else:
            opp_copy(n, size).wait_send()
            for w in range(2):
                all_copy(n, w, size).wait_send()
        for o in (1, 2, 3):
            sec_copy(n, o, size).wait_send()

    def unit(n, lag, act):
        m = n - lag

        for k in range(PARTS):

            @pl.when((m >= k * NCH) & (m < k * NCH + NCH))
            def _():
                act(m, k)

    def contract_x(i):
        parts = [nn(cxp[...], gath[i, m]).reshape(8, 24, T) for m in range(len(PIECES[i]))]
        if i == THIRD:
            parts.append(g3[...].reshape(8, 12, T))
        used = sum(p.shape[1] for p in parts)
        if used < lines(i):
            parts.append(jnp.zeros((8, lines(i) - used, T), F32))
        hbuf[i, :, 0 : lines(i), :] = jnp.concatenate(parts, axis=1).astype(BF16)
        for k in (4, 3, 5, 2, 6, 1, 7):
            z_copy(i, k).start()

    def finish_z(i):
        for k in range(1, 8):
            z_copy(i, k).wait_recv()
        tot = hbuf[i, z, 0 : lines(i), :].astype(F32)
        for k in range(7):
            tot = tot + zrecv[i, k, 0 : lines(i), :].astype(F32)
        for m in range(slabs(i)):
            each = 6 if m < len(PIECES[i]) else 3
            for q in range(4):
                at = m * 24 + q * each
                fbuf[i, q, m, 0:each] = tot[at : at + each]
        for k in (1, 2, 3):
            f_copy(i, k).start()

    def modes_a():
        high = lax.Precision.HIGHEST
        one = nn(pick(T, T, lambda q: 16 * ((q >> 1) & 7) + 2 * (q >> 4) + (q & 1), F32), g1[...], high)
        two = nn(pick(T, T, lambda q: 32 * ((q >> 2) & 3) + 4 * (q >> 4) + (q & 3), F32), g2[...], high)
        m12[:, 0:16, :] = one.reshape(8, 16, T).astype(BF16)
        m12[:, 16:32, :] = two.reshape(8, 16, T).astype(BF16)
        for k in range(1, 8):
            ma_copy(k).start()

    def modes_b():
        total = m12[g].astype(F32)
        for k in range(1, 8):
            ma_copy(k).wait_recv()
            total = total + arecv[k - 1].astype(F32)

        def source_row(q):
            i = q & 7
            low = jnp.where(i < 2, 2 * (q >> 3) + i, -1)
            return jnp.where(q < 64, low, jnp.where(i < 4, 16 + 4 * ((q - 64) >> 3) + i, -1))

        msg[...] = nn(pick(96, 32, source_row, F32), total, lax.Precision.HIGHEST).reshape(12, 8, T)
        for k in range(1, 8):
            mb_copy(k).start()
        for b in range(4):

            @pl.when(v * 4 + b != t)
            def _():
                mc_send(b).start()

            @pl.when(v * 4 + b == t)
            def _():
                r2[u] = msg[8 + b]

    def turn(n, _):
        @pl.when(n < NCH)
        def _():
            contract_z(n)

        @pl.when(n == MODE_0 - 1)
        def _():
            prepare()

        unit(n, 0, contract_y)
        unit(n, DIRECT, direct)
        unit(n, FORWARD, forward)

        @pl.when((n >= MODE_0) & (n < MODE_0 + T // MODE))
        def _():
            modes(n - MODE_0)

        unit(n, FINISH, finish)
        unit(n, COLLECT, collect)

        for i in range(PARTS):
            last = NCH * i + NCH - 1 + COLLECT

            @pl.when(n == last)
            def _():
                contract_x(i)

            if last + ZLAG < UNITS + COLLECT:

                @pl.when(n == last + ZLAG)
                def _():
                    finish_z(i)

        @pl.when(n == MODE_A)
        def _():
            modes_a()

        @pl.when(n == MODE_B)
        def _():
            modes_b()

        return 0

    lax.fori_loop(0, UNITS + COLLECT, turn, 0)

    def sent(n, _):
        unit(n, 0, drain)
        return 0

    lax.fori_loop(0, UNITS, sent, 0)
    for ch in range(NCH):
        par_copy(ch).wait_send()
    for k in range(1, 8):
        ma_copy(k).wait_send()

    def place_rows(i):
        for m, (kind, index) in enumerate(PIECES[i]):
            out[s * 9 + kind * 3 + index] = fbuf[i, s, m]
        for k in (1, 2, 3):
            f_copy(i, k).wait_recv()
            for m, (kind, index) in enumerate(PIECES[i]):
                out[step(s, 4 - k) * 9 + kind * 3 + index] = frecv[i, k - 1, m]
        if i == THIRD:
            at = len(PIECES[i])
            out[36] = fbuf[i, s, at] + frecv[i, 0, at] + frecv[i, 1, at] + frecv[i, 2, at]

    def drain_rows(i):
        for k in range(1, 8):
            z_copy(i, k).wait_send()
        for k in (1, 2, 3):
            f_copy(i, k).wait_send()

    for i in range(PARTS - 1):
        if NCH * i + NCH - 1 + ZLAG >= UNITS:
            finish_z(i)

    first = msg[v]
    for k in range(1, 8):
        mb_copy(k).wait_recv()
        first = first + r1[k - 1]
    out[37] = first
    for k in range(4):

        @pl.when(k * 8 + lax.div(t, 4) != t)
        def _():
            mc_recv(k).wait_recv()

    out[38] = r2[0] + r2[1] + r2[2] + r2[3]
    for k in range(1, 8):
        mb_copy(k).wait_send()
    for b in range(4):

        @pl.when(v * 4 + b != t)
        def _():
            mc_send(b).wait_send()

    for i in range(PARTS - 1):
        place_rows(i)
        drain_rows(i)
    finish_z(PARTS - 1)
    place_rows(PARTS - 1)
    drain_rows(PARTS - 1)


def outputs_kernel(x, one, two, three, core):
    one[...] = x[37 * 8 : 37 * 8 + 2, 0:K]
    two[...] = x[38 * 8 : 38 * 8 + 4, 0:K]
    three[...] = x[36 * 8 : 36 * 8 + 3, :]
    for p in range(6):
        rows = x[pl.ds(p, 36, stride=8), :]
        for q in range(4):
            core[p, 6 * q : 6 * q + 6, 0:128] = rows[9 * q : 9 * q + 6]
            core[p, 6 * q : 6 * q + 3, 128:192] = rows[9 * q + 6 : 9 * q + 9, 0:64]
            core[p, 6 * q + 3 : 6 * q + 6, 128:192] = rows[9 * q + 6 : 9 * q + 9, 64:128]


def shards(field, *small):
    vm, hbm = pl.BlockSpec(memory_space=pltpu.VMEM), pl.BlockSpec(memory_space=pl.ANY)
    dma, mem = pltpu.SemaphoreType.DMA, pltpu.VMEM
    unit = [dma((UNITS, 2))] * 6 + [dma((UNITS, 3))] * 2
    raw = pl.pallas_call(
        main_kernel,
        out_shape=jax.ShapeDtypeStruct((39, 8, 128), F32),
        in_specs=[hbm] * 10,
        out_specs=vm,
        scratch_shapes=[
            mem((NCH, CH, T, T), BF16),
            mem((NCH, CH, T, T), BF16),
            mem((2, 3, NCH, CH * 16, 256), BF16),
            mem((CH * 16 * MOST, 128), F32),
            mem((UNITS, 16, ROWS, 128), BF16),
            mem((UNITS, 4, ROWS, 128), BF16),
            mem((UNITS, 2, 4, ROWS, 128), BF16),
            mem((UNITS, 3, ROWS, 128), BF16),
            mem((PARTS, MOST, T, 128), BF16),
            mem((PARTS, 8, 32 * MOST + 32, 128), BF16),
            mem((PARTS, 7, 32 * MOST + 32, 128), BF16),
            mem((PARTS, 4, MOST + 1, 8, 128), F32),
            mem((PARTS, 3, MOST + 1, 8, 128), F32),
            mem((S, T), BF16), mem((2, S, T), BF16), mem((S, T), BF16),
            mem((K, T), BF16), mem((K, T), BF16), mem((K, T), BF16), mem((K, T), BF16),
            mem((K, T), BF16), mem((K, T), BF16),
            mem((K, T), BF16),
            mem((S, T), BF16),
            mem((2, 2 * T, 256), BF16),
            mem((T, 256), BF16),
            mem((T, 128), F32), mem((T, 128), F32),
            mem((T // MODE, K, 128), F32),
            mem((T, 128), F32), mem((T, 128), F32), mem((K, T), F32),
            mem((8, 32, 128), BF16), mem((7, 32, 128), BF16),
            mem((12, 8, 128), F32), mem((7, 8, 128), F32), mem((4, 8, 128), F32),
            dma((10,)), dma((NCH,)), dma((NCH,)), dma((NCH,)),
            *unit,
            dma((PARTS, 7)), dma((PARTS, 7)), dma((PARTS, 3)), dma((PARTS, 3)),
            dma((7,)), dma((7,)), dma((7,)), dma((7,)), dma((4,)), dma((4,)),
        ],
        compiler_params=pltpu.CompilerParams(
            collective_id=0, has_side_effects=True, vmem_limit_bytes=56 * 1024 * 1024
        ),
    )(field, *[x.T for x in small])
    one, two, three, core = pl.pallas_call(
        outputs_kernel,
        out_shape=(
            jax.ShapeDtypeStruct((2, K), F32),
            jax.ShapeDtypeStruct((4, K), F32),
            jax.ShapeDtypeStruct((3, T), F32),
            jax.ShapeDtypeStruct((6, 24, S), F32),
        ),
        in_specs=[vm],
        out_specs=(vm, vm, vm, vm),
    )(raw.reshape(39 * 8, 128))
    return (one, two, three, core.transpose(0, 2, 1))


def solution(mesh):
    return jax.shard_map(
        shards,
        mesh=mesh,
        in_specs=(
            P("xy", None, None, "gz"),
            P(), P(), P("gz", None), P(), P(), P(), P(), P("gz", None), P("gz", None),
        ),
        out_specs=(
            P(("xy", "gz"), None),
            P(("xy", "gz"), None),
            P("xy", "gz"),
            P("xy", None, "gz"),
        ),
        check_vma=False,
    )
```

time: 65 us -> 64.2 us (0.988)
  Pallas kernels: 64.2 us -> 63.5 us
    pallas_call x1, Pallas kernels: 62.5 us -> 61.8 us  [shards(): pl.pallas_call(main_kernel, out_shape=jax.ShapeDtypeStruct((39, 8, 128),...]
where the time goes in v4:
time: 64.2 us; the launch traced here: 64.1 us
  Pallas kernels  63.5 us (99%)
    pallas_call x1, Pallas kernels, shards(): pl.pallas_call(main_kernel, out_shape=jax.ShapeDtypeStruct((39, 8, 128),...  61.8 us
    pallas_call x1, Pallas kernels, shards(): pl.pallas_call(outputs_kernel, out_shape=(jax.ShapeDtypeStruct((2, K), F3...  1.68 us

profile of v4, /device:TPU:1, one launch (start us, length us, event | category | flops | bytes accessed | tf_op | source)
XLA Modules:
  0.0 64.1 jit_solution(16697935436025334763)
XLA Ops:
  0.6 61.8 %shard_map.129 = f32[39,8,128]{2,1,0:T(8,128)} custom-call(bf16[1,128,128,128]{3,2,1,0:T(8,128)(2,1)} %field.1, bf16[192,512]{1,0:T(8,128)(2,1)} %bitcast.13, bf16[192,1024]{1,0:T(8,128)(2,1)} %bitcast.12, bf16[192,128]{1,0:T(8,128)(2,1)} %bitcast.18, bf16[96,512]{1,0:T(8,128)(2,1)} %bitcast.16, bf16[96,512]{1,0:T(8,128)(2,1)} %bitcast.17, ...), custom_call_target="tpu_custom_call" | custom-call | tf_op jit(solution)/shard_map/pallas_call | solution.py:532
  62.5 1.7 %shard_map.130 = (f32[2,96]{1,0:T(2,128)}, f32[4,96]{1,0:T(4,128)}, f32[3,128]{1,0:T(4,128)}, f32[6,24,192]{2,1,0:T(8,128)}) custom-call(f32[312,128]{1,0:T(8,128)} %bitcast.11), custom_call_target="tpu_custom_call" | custom-call | tf_op jit(solution)/shard_map/pallas_call | solution.py:572

commit v5 on v4

--- a/solution.py
+++ b/solution.py
@@ -19,8 +19,8 @@
 MOST = 3
 ROWS = MOST * CH
 MODE = 16
-DIRECT, FORWARD, FINISH, COLLECT, ZLAG = 1, 2, 5, 8, 6
-MODE_0, MODE_A, MODE_B = 4, 12, 16
+DIRECT, FORWARD, FINISH, COLLECT, ZLAG = 1, 2, 5, 8, 5
+MODE_0, MODE_A, MODE_B = 5, 13, 16
 
 
 def nn(a, b, precision=None):

time: 64.2 us -> 63.7 us (level)
  no operation moved by 1% of the time
where the time goes in v5:
time: 63.7 us; the launch traced here: 63.6 us
  Pallas kernels  63 us (99%)
  between operations  0.64 us (1%)
    pallas_call x1, Pallas kernels, shards(): pl.pallas_call(main_kernel, out_shape=jax.ShapeDtypeStruct((39, 8, 128),...  61.3 us
    pallas_call x1, Pallas kernels, shards(): pl.pallas_call(outputs_kernel, out_shape=(jax.ShapeDtypeStruct((2, K), F3...  1.68 us

profile of v5, /device:TPU:1, one launch (start us, length us, event | category | flops | bytes accessed | tf_op | source)
XLA Modules:
  0.0 63.6 jit_solution(4962279879650548764)
XLA Ops:
  0.6 61.3 %shard_map.129 = f32[39,8,128]{2,1,0:T(8,128)} custom-call(bf16[1,128,128,128]{3,2,1,0:T(8,128)(2,1)} %field.1, bf16[192,512]{1,0:T(8,128)(2,1)} %bitcast.13, bf16[192,1024]{1,0:T(8,128)(2,1)} %bitcast.12, bf16[192,128]{1,0:T(8,128)(2,1)} %bitcast.18, bf16[96,512]{1,0:T(8,128)(2,1)} %bitcast.16, bf16[96,512]{1,0:T(8,128)(2,1)} %bitcast.17, ...), custom_call_target="tpu_custom_call" | custom-call | tf_op jit(solution)/shard_map/pallas_call | solution.py:532
  61.9 1.7 %shard_map.130 = (f32[2,96]{1,0:T(2,128)}, f32[4,96]{1,0:T(4,128)}, f32[3,128]{1,0:T(4,128)}, f32[6,24,192]{2,1,0:T(8,128)}) custom-call(f32[312,128]{1,0:T(8,128)} %bitcast.11), custom_call_target="tpu_custom_call" | custom-call | tf_op jit(solution)/shard_map/pallas_call | solution.py:572

commit v6 on v5

--- a/solution.py
+++ b/solution.py
@@ -422,12 +422,12 @@
         unit(n, DIRECT, direct)
         unit(n, FORWARD, forward)
 
-        @pl.when((n >= MODE_0) & (n < MODE_0 + T // MODE))
-        def _():
-            modes(n - MODE_0)
-
         unit(n, FINISH, finish)
         unit(n, COLLECT, collect)
+
+        @pl.when((n >= MODE_0) & (n < MODE_0 + T // MODE))
+        def _():
+            modes(n - MODE_0)
 
         for i in range(PARTS):
             last = NCH * i + NCH - 1 + COLLECT

time: 63.7 us -> 63.8 us (level)
  no operation moved by 1% of the time
where the time goes in v6:
time: 63.8 us; the launch traced here: 63.7 us
  Pallas kernels  63 us (99%)
  between operations  0.64 us (1%)
    pallas_call x1, Pallas kernels, shards(): pl.pallas_call(main_kernel, out_shape=jax.ShapeDtypeStruct((39, 8, 128),...  61.3 us
    pallas_call x1, Pallas kernels, shards(): pl.pallas_call(outputs_kernel, out_shape=(jax.ShapeDtypeStruct((2, K), F3...  1.68 us

profile of v6, /device:TPU:1, one launch (start us, length us, event | category | flops | bytes accessed | tf_op | source)
XLA Modules:
  0.0 63.7 jit_solution(2141260896140075100)
XLA Ops:
  0.6 61.3 %shard_map.129 = f32[39,8,128]{2,1,0:T(8,128)} custom-call(bf16[1,128,128,128]{3,2,1,0:T(8,128)(2,1)} %field.1, bf16[192,512]{1,0:T(8,128)(2,1)} %bitcast.13, bf16[192,1024]{1,0:T(8,128)(2,1)} %bitcast.12, bf16[192,128]{1,0:T(8,128)(2,1)} %bitcast.18, bf16[96,512]{1,0:T(8,128)(2,1)} %bitcast.16, bf16[96,512]{1,0:T(8,128)(2,1)} %bitcast.17, ...), custom_call_target="tpu_custom_call" | custom-call | tf_op jit(solution)/shard_map/pallas_call | solution.py:532
  62.0 1.7 %shard_map.130 = (f32[2,96]{1,0:T(2,128)}, f32[4,96]{1,0:T(4,128)}, f32[3,128]{1,0:T(4,128)}, f32[6,24,192]{2,1,0:T(8,128)}) custom-call(f32[312,128]{1,0:T(8,128)} %bitcast.11), custom_call_target="tpu_custom_call" | custom-call | tf_op jit(solution)/shard_map/pallas_call | solution.py:572
